TPU v7x, 256 devices: a whole 4x4x8 slice. The times are simulated.
256 devices in a mesh: rows: 128 (over z, y, x), feat: 2 (over core).
Axes of the slice: x: 4, y: 4, z: 8, core: 2. Of those that a mesh axis runs over, the one named last changes fastest.
Arguments:
- student: bfloat16 [40960, 1024], P('rows', 'feat')
- teacher: bfloat16 [40960, 1536], P('rows', 'feat')
- rounds: int32 [4], replicated, may hold values from 1 to 127
Outputs:
- student_grad: float32 [40960, 1024], P('rows', 'feat')
- loss: float32 [], replicated
Inputs may be any that keep to these rules, and one draw needn't show every extreme that they name: Round r pairs block b with block b XOR rounds[r].
All inputs are finite; a program needn't handle non-finite values.
Results may differ from a plain program's by a relative error of at most 0.018.
Values may be sent and summed in bfloat16 or wider, within the bound.
A program may use at most 64 MiB of HBM per device.

v0:
```python
import jax
import jax.numpy as jnp
from jax import lax
from jax.sharding import PartitionSpec as P


def swapped_2(value, axis, apart):
    mask = 2**apart
    pairs = [(source, source ^ mask) for source in range(lax.axis_size(axis))]
    return lax.ppermute(value, axis, pairs)


def body(student, teacher, rounds):
    half_s = student.shape[1]
    own_rows = student.shape[0]
    round_count = rounds.shape[0]
    level_count = lax.axis_size("rows").bit_length() - 1
    pair_count = float(lax.axis_size("rows") * (round_count + 1) * own_rows * own_rows)
    joined = jnp.concatenate([student, teacher], axis=1)
    mate_blocks = [joined]
    for turn in range(round_count):
        current = joined
        for level in range(level_count):
            take = rounds[turn] >> level & 1 == 1
            swapped = swapped_2(current, "rows", level)
            current = jnp.where(take, swapped, current)
        mate_blocks.append(current)
    tiles_s = []
    tiles_t = []
    mate_halves = []
    total_s = jnp.zeros((), jnp.float32)
    total_t = jnp.zeros((), jnp.float32)
    own_sq_s = None
    own_sq_t = None
    full_own_s = None
    full_own_t = None
    for slot in range(round_count + 1):
        mate_s = mate_blocks[slot][:, :half_s]
        mate_t = mate_blocks[slot][:, half_s:]
        mate_halves.append(mate_s)
        wide_s, wide_t = (
            lax.all_gather(mate_s, "feat", axis=1, tiled=True),
            lax.all_gather(mate_t, "feat", axis=1, tiled=True),
        )
        mate_sq_s = jnp.sum(wide_s.astype(jnp.float32) ** 2, axis=1)
        mate_sq_t = jnp.sum(wide_t.astype(jnp.float32) ** 2, axis=1)
        if slot == 0:
            full_own_s, full_own_t = (wide_s, wide_t)
            own_sq_s, own_sq_t = (mate_sq_s, mate_sq_t)
        inner_s = jnp.dot(full_own_s, wide_s.T, preferred_element_type=jnp.float32)
        inner_t = jnp.dot(full_own_t, wide_t.T, preferred_element_type=jnp.float32)
        dist_s = jnp.sqrt(own_sq_s[:, None] + mate_sq_s[None, :] - 2.0 * inner_s + 1.0)
        dist_t = jnp.sqrt(own_sq_t[:, None] + mate_sq_t[None, :] - 2.0 * inner_t + 1.0)
        tiles_s.append(dist_s)
        tiles_t.append(dist_t)
        total_s = total_s + jnp.sum(dist_s)
        total_t = total_t + jnp.sum(dist_t)
    total_s, total_t = lax.psum((total_s, total_t), "rows")
    mean_s = total_s / pair_count
    mean_t = total_t / pair_count
    slopes = []
    local_h = jnp.zeros((), jnp.float32)
    local_g = jnp.zeros((), jnp.float32)
    for slot in range(round_count + 1):
        err = tiles_s[slot] / mean_s - tiles_t[slot] / mean_t
        huber = jnp.where(jnp.abs(err) < 1.0, 0.5 * err * err, jnp.abs(err) - 0.5)
        slope = jnp.clip(err, -1.0, 1.0)
        slopes.append(slope)
        local_h = local_h + jnp.sum(huber)
        local_g = local_g + jnp.sum(slope * tiles_s[slot])
    total_h, total_g = lax.psum((local_h, local_g), "rows")
    loss = total_h / pair_count
    kappa = total_g / (mean_s * pair_count)
    own_float = student.astype(jnp.float32)
    grad = jnp.zeros((own_rows, half_s), jnp.float32)
    for slot in range(round_count + 1):
        weight = (slopes[slot] - kappa) / tiles_s[slot]
        row_total = jnp.sum(weight, axis=1)
        pulled = jnp.dot(
            weight.astype(jnp.bfloat16), mate_halves[slot], preferred_element_type=jnp.float32
        )
        grad = grad + row_total[:, None] * own_float - pulled
    return (2.0 * grad, loss)


def solution(mesh):
    return jax.shard_map(
        body,
        mesh=mesh,
        in_specs=(P("rows", "feat"), P("rows", "feat"), P()),
        out_specs=(P("rows", "feat"), P()),
        check_vma=False,
    )
```

profile of v0, /device:TPU:2, one launch (start us, length us, event | category | flops | bytes accessed | tf_op | source)
XLA Modules:
  0.0 1610.7 jit_solution(14445656292218455034)
XLA Ops:
  2.8 2.4 collective-permute-start
  23.7 2.3 all_gather.30
  25.9 2.5 all_gather.35
  30.0 2.1 fusion.74
  32.1 2.8 collective-permute-start.1
  34.9 2.1 fusion.79
  37.7 2.8 collective-permute-start.13
  40.5 10.8 collective-permute-done.19
  51.5 17.4 %collective-permute-done.1 = bf16[320,1280]{1,0:T(8,128)(2,1)S(1)} collective-permute-done((bf16[320,1280]{1,0:T(8,128)(2,1)S(1)}, bf16[320,1280]{1,0:T(8,128)(2,1)S(1)}, u32[]{:S(2)}, u32[]{:S(2)}) %collective-permute-start.1) | collective-permute-done | bytes 819232 | tf_op jit(solution)/shard_map/ppermute | solution.py:10
  69.1 17.4 %collective-permute-done.7 = bf16[320,1280]{1,0:T(8,128)(2,1)S(1)} collective-permute-done((bf16[320,1280]{1,0:T(8,128)(2,1)S(1)}, bf16[320,1280]{1,0:T(8,128)(2,1)S(1)}, u32[]{:S(2)}, u32[]{:S(2)}) %collective-permute-start.7) | collective-permute-done | bytes 819232 | tf_op jit(solution)/shard_map/ppermute | solution.py:10
  86.6 16.6 %collective-permute-done.13 = bf16[320,1280]{1,0:T(8,128)(2,1)S(1)} collective-permute-done((bf16[320,1280]{1,0:T(8,128)(2,1)S(1)}, bf16[320,1280]{1,0:T(8,128)(2,1)S(1)}, u32[]{:S(2)}, u32[]{:S(2)}) %collective-permute-start.13) | collective-permute-done | bytes 819232 | tf_op jit(solution)/shard_map/ppermute | solution.py:10
  103.5 2.8 collective-permute-start.21
  107.5 2.8 collective-permute-start.9
  110.3 14.3 collective-permute-done.14
  124.7 1.5 collective-permute-start.15
  126.2 16.6 %collective-permute-done.21 = bf16[320,1280]{1,0:T(8,128)(2,1)S(1)} collective-permute-done((bf16[320,1280]{1,0:T(8,128)(2,1)S(1)}, bf16[320,1280]{1,0:T(8,128)(2,1)S(1)}, u32[]{:S(2)}, u32[]{:S(2)}) %collective-permute-start.21) | collective-permute-done | bytes 819232 | tf_op jit(solution)/shard_map/ppermute | solution.py:10
  143.0 2.0 collective-permute-start.22
  145.0 15.4 collective-permute-done.3
  160.5 2.0 collective-permute-start.4
  162.5 15.4 collective-permute-done.9
  178.1 2.2 collective-permute-start.10
  180.2 13.5 collective-permute-done.15
  193.9 2.0 collective-permute-start.16
  196.0 3.4 collective-permute-start.23
  199.7 3.0 collective-permute-start.11
  202.7 27.5 %collective-permute-done.16 = bf16[320,1280]{1,0:T(8,128)(2,1)S(1)} collective-permute-done((bf16[320,1280]{1,0:T(8,128)(2,1)S(1)}, bf16[320,1280]{1,0:T(8,128)(2,1)S(1)}, u32[]{:S(2)}, u32[]{:S(2)}) %collective-permute-start.16) | collective-permute-done | bytes 819232 | tf_op jit(solution)/shard_map/ppermute | solution.py:10
  231.4 74.9 %collective-permute-done.23 = bf16[320,1280]{1,0:T(8,128)(2,1)S(1)} collective-permute-done((bf16[320,1280]{1,0:T(8,128)(2,1)S(1)}, bf16[320,1280]{1,0:T(8,128)(2,1)S(1)}, u32[]{:S(2)}, u32[]{:S(2)}) %collective-permute-start.23) | collective-permute-done | bytes 819232 | tf_op jit(solution)/shard_map/ppermute | solution.py:10
  306.4 6.0 collective-permute-start.24
  312.4 20.4 %collective-permute-done.5 = bf16[320,1280]{1,0:T(8,128)(2,1)S(1)} collective-permute-done((bf16[320,1280]{1,0:T(8,128)(2,1)S(1)}, bf16[320,1280]{1,0:T(8,128)(2,1)S(1)}, u32[]{:S(2)}, u32[]{:S(2)}) %collective-permute-start.5) | collective-permute-done | bytes 819232 | tf_op jit(solution)/shard_map/ppermute | solution.py:10
  333.0 14.9 collective-permute-start.6
  347.9 20.4 %collective-permute-done.11 = bf16[320,1280]{1,0:T(8,128)(2,1)S(1)} collective-permute-done((bf16[320,1280]{1,0:T(8,128)(2,1)S(1)}, bf16[320,1280]{1,0:T(8,128)(2,1)S(1)}, u32[]{:S(2)}, u32[]{:S(2)}) %collective-permute-start.11) | collective-permute-done | bytes 819232 | tf_op jit(solution)/shard_map/ppermute | solution.py:10
  368.4 14.9 collective-permute-start.12
  383.4 17.7 %collective-permute-done.17 = bf16[320,1280]{1,0:T(8,128)(2,1)S(1)} collective-permute-done((bf16[320,1280]{1,0:T(8,128)(2,1)S(1)}, bf16[320,1280]{1,0:T(8,128)(2,1)S(1)}, u32[]{:S(2)}, u32[]{:S(2)}) %collective-permute-start.17) | collective-permute-done | bytes 819232 | tf_op jit(solution)/shard_map/ppermute | solution.py:10
  401.2 83.9 %collective-permute-start.18 = (bf16[320,1280]{1,0:T(8,128)(2,1)S(1)}, bf16[320,1280]{1,0:T(8,128)(2,1)S(1)}, u32[]{:S(2)}, u32[]{:S(2)}) collective-permute-start(bf16[320,1280]{1,0:T(8,128)(2,1)S(1)} %broadcast_select_fusion.12), channel_id=1, source_target_pairs={{0,128},{2,130},{4,132},{6,134},{8,136},{10,138},{12,140},{14,142}... | collective-permute-start | bytes 2457608 | tf_op jit(solution)/shard_map/ppermute | solution.py:10
  486.6 17.8 %collective-permute-done.18 = bf16[320,1280]{1,0:T(8,128)(2,1)S(1)} collective-permute-done((bf16[320,1280]{1,0:T(8,128)(2,1)S(1)}, bf16[320,1280]{1,0:T(8,128)(2,1)S(1)}, u32[]{:S(2)}, u32[]{:S(2)}) %collective-permute-start.18) | collective-permute-done | bytes 819232 | tf_op jit(solution)/shard_map/ppermute | solution.py:10
  504.5 1.2 slice-done.4
  505.7 2.3 all_gather.34
  508.2 1.3 fusion.83
  509.5 2.5 all_gather.39
  512.2 2.2 fusion.78
  514.5 2.5 all_gather.36
  517.2 2.2 fusion.75
  519.4 2.5 all_gather.37
  522.2 2.2 fusion.76
  524.5 2.5 all_gather.38
  527.3 2.2 fusion.77
  529.4 2.3 all_gather.31
  531.9 1.3 fusion.80
  533.3 2.5 all_gather.32
  536.0 2.0 fusion.81
  538.0 2.3 all_gather.33
  540.5 2.1 fusion.82
  548.9 344.2 %all-reduce = (f32[]{:T(128)}, f32[]{:T(128)}) all-reduce(f32[]{:T(128)S(6)} %add.256, f32[]{:T(128)S(6)} %add.236), channel_id=1, replica_groups=mesh['rows'=128,'feat'=2] {'rows'}, use_global_device_ids=true, to_apply=%region_21.22 | all-reduce | flops 2 | bytes 16 | tf_op jit(solution)/shard_map/psum | solution.py:58
  894.3 1.8 multiply_reduce_fusion.10
  896.1 1.5 multiply_reduce_fusion.14
  899.8 1.5 multiply_reduce_fusion.12
  902.0 2.7 multiply_reduce_fusion.11
  906.0 343.1 %psum.30 = f32[]{:T(128)} all-reduce(f32[]{:T(128)S(6)} %add.260), channel_id=1, replica_groups=mesh['rows'=128,'feat'=2] {'rows'}, use_global_device_ids=true, to_apply=%region_27.28 | all-reduce | flops 1 | bytes 8 | tf_op jit(solution)/shard_map/psum | solution.py:71
  1250.4 1.2 fusion.56
  1252.8 1.2 fusion.58
  1259.2 2.2 fusion.60
  1261.4 344.1 %psum.31 = f32[]{:T(128)} all-reduce(f32[]{:T(128)S(6)} %add.268), channel_id=1, replica_groups=mesh['rows'=128,'feat'=2] {'rows'}, use_global_device_ids=true, to_apply=%region_38.39 | all-reduce | flops 1 | bytes 8 | tf_op jit(solution)/shard_map/psum | solution.py:71
  1606.3 1.6 fusion.7
  1608.1 1.4 fusion.6
  (130 shorter events, 17.5 us)
Async XLA Ops:
  0.6 23.0 %copy-start.8 = (bf16[320,512]{1,0:T(8,128)(2,1)S(1)}, bf16[320,512]{1,0:T(8,128)(2,1)}, u32[]{:S(2)}) copy-start(bf16[320,512]{1,0:T(8,128)(2,1)} %param.3) | copy-start | bytes 983044
  0.6 4.6 copy-start.26
  1.7 24.2 %copy-start.11 = (bf16[320,768]{1,0:T(8,128)(2,1)S(1)}, bf16[320,768]{1,0:T(8,128)(2,1)}, u32[]{:S(2)}) copy-start(bf16[320,768]{1,0:T(8,128)(2,1)} %param.4) | copy-start | bytes 1474564
  2.8 25.6 %collective-permute-start = (bf16[320,1280]{1,0:T(8,128)(2,1)S(1)}, bf16[320,1280]{1,0:T(8,128)(2,1)S(1)}, u32[]{:S(2)}, u32[]{:S(2)}) collective-permute-start(bf16[320,1280]{1,0:T(8,128)(2,1)S(1)} %constant_dynamic-update-slice_fusion), channel_id=1, source_target_pairs={{0,2},{2,0},{4,6},{6,4},{8,10},{10,8},{12,14},{14,12},{16,18},{18,... | collective-permute-start | bytes 2457608 | tf_op jit(solution)/shard_map/ppermute | solution.py:10
  28.7 22.7 %collective-permute-start.19 = (bf16[320,1280]{1,0:T(8,128)(2,1)S(1)}, bf16[320,1280]{1,0:T(8,128)(2,1)S(1)}, u32[]{:S(2)}, u32[]{:S(2)}) collective-permute-start(bf16[320,1280]{1,0:T(8,128)(2,1)S(1)} %get-tuple-element.25), channel_id=1, source_target_pairs={{0,4},{2,6},{4,0},{6,2},{8,12},{10,14},{12,8},{14,10},{16,20},{18,... | collective-permute-start | bytes 2457608 | tf_op jit(solution)/shard_map/ppermute | solution.py:10
  32.1 36.8 %collective-permute-start.1 = (bf16[320,1280]{1,0:T(8,128)(2,1)S(1)}, bf16[320,1280]{1,0:T(8,128)(2,1)S(1)}, u32[]{:S(2)}, u32[]{:S(2)}) collective-permute-start(bf16[320,1280]{1,0:T(8,128)(2,1)S(1)} %get-tuple-element.27), channel_id=1, source_target_pairs={{0,4},{2,6},{4,0},{6,2},{8,12},{10,14},{12,8},{14,10},{16,20},{18,... | collective-permute-start | bytes 2457608 | tf_op jit(solution)/shard_map/ppermute | solution.py:10
  37.0 49.4 %collective-permute-start.7 = (bf16[320,1280]{1,0:T(8,128)(2,1)S(1)}, bf16[320,1280]{1,0:T(8,128)(2,1)S(1)}, u32[]{:S(2)}, u32[]{:S(2)}) collective-permute-start(bf16[320,1280]{1,0:T(8,128)(2,1)S(1)} %get-tuple-element.26), channel_id=1, source_target_pairs={{0,4},{2,6},{4,0},{6,2},{8,12},{10,14},{12,8},{14,10},{16,20},{18,... | collective-permute-start | bytes 2457608 | tf_op jit(solution)/shard_map/ppermute | solution.py:10
  37.7 65.5 %collective-permute-start.13 = (bf16[320,1280]{1,0:T(8,128)(2,1)S(1)}, bf16[320,1280]{1,0:T(8,128)(2,1)S(1)}, u32[]{:S(2)}, u32[]{:S(2)}) collective-permute-start(bf16[320,1280]{1,0:T(8,128)(2,1)S(1)} %get-tuple-element.24), channel_id=1, source_target_pairs={{0,4},{2,6},{4,0},{6,2},{8,12},{10,14},{12,8},{14,10},{16,20},{18,... | collective-permute-start | bytes 2457608 | tf_op jit(solution)/shard_map/ppermute | solution.py:10
  51.4 52.0 %collective-permute-start.20 = (bf16[320,1280]{1,0:T(8,128)(2,1)S(1)}, bf16[320,1280]{1,0:T(8,128)(2,1)S(1)}, u32[]{:S(2)}, u32[]{:S(2)}) collective-permute-start(bf16[320,1280]{1,0:T(8,128)(2,1)S(1)} %broadcast_select_fusion.1), channel_id=1, source_target_pairs={{0,8},{2,10},{4,12},{6,14},{8,0},{10,2},{12,4},{14,6},{16,24},{18,... | collective-permute-start | bytes 2457608 | tf_op jit(solution)/shard_map/ppermute | solution.py:10
  69.0 37.3 %collective-permute-start.2 = (bf16[320,1280]{1,0:T(8,128)(2,1)S(1)}, bf16[320,1280]{1,0:T(8,128)(2,1)S(1)}, u32[]{:S(2)}, u32[]{:S(2)}) collective-permute-start(bf16[320,1280]{1,0:T(8,128)(2,1)S(1)} %broadcast_select_fusion.22), channel_id=1, source_target_pairs={{0,8},{2,10},{4,12},{6,14},{8,0},{10,2},{12,4},{14,6},{16,24},{18,... | collective-permute-start | bytes 2457608 | tf_op jit(solution)/shard_map/ppermute | solution.py:10
  86.5 20.8 %collective-permute-start.8 = (bf16[320,1280]{1,0:T(8,128)(2,1)S(1)}, bf16[320,1280]{1,0:T(8,128)(2,1)S(1)}, u32[]{:S(2)}, u32[]{:S(2)}) collective-permute-start(bf16[320,1280]{1,0:T(8,128)(2,1)S(1)} %broadcast_select_fusion.15), channel_id=1, source_target_pairs={{0,8},{2,10},{4,12},{6,14},{8,0},{10,2},{12,4},{14,6},{16,24},{18,... | collective-permute-start | bytes 2457608 | tf_op jit(solution)/shard_map/ppermute | solution.py:10
  103.3 21.3 %collective-permute-start.14 = (bf16[320,1280]{1,0:T(8,128)(2,1)S(1)}, bf16[320,1280]{1,0:T(8,128)(2,1)S(1)}, u32[]{:S(2)}, u32[]{:S(2)}) collective-permute-start(bf16[320,1280]{1,0:T(8,128)(2,1)S(1)} %broadcast_select_fusion.8), channel_id=1, source_target_pairs={{0,8},{2,10},{4,12},{6,14},{8,0},{10,2},{12,4},{14,6},{16,24},{18,... | collective-permute-start | bytes 2457608 | tf_op jit(solution)/shard_map/ppermute | solution.py:10
  103.5 39.3 %collective-permute-start.21 = (bf16[320,1280]{1,0:T(8,128)(2,1)S(1)}, bf16[320,1280]{1,0:T(8,128)(2,1)S(1)}, u32[]{:S(2)}, u32[]{:S(2)}) collective-permute-start(bf16[320,1280]{1,0:T(8,128)(2,1)S(1)} %broadcast_select_fusion.2), channel_id=1, source_target_pairs={{0,16},{2,18},{4,20},{6,22},{8,24},{10,26},{12,28},{14,30},{16,0},... | collective-permute-start | bytes 2457608 | tf_op jit(solution)/shard_map/ppermute | solution.py:10
  106.4 53.9 %collective-permute-start.3 = (bf16[320,1280]{1,0:T(8,128)(2,1)S(1)}, bf16[320,1280]{1,0:T(8,128)(2,1)S(1)}, u32[]{:S(2)}, u32[]{:S(2)}) collective-permute-start(bf16[320,1280]{1,0:T(8,128)(2,1)S(1)} %broadcast_select_fusion.23), channel_id=1, source_target_pairs={{0,16},{2,18},{4,20},{6,22},{8,24},{10,26},{12,28},{14,30},{16,0},... | collective-permute-start | bytes 2457608 | tf_op jit(solution)/shard_map/ppermute | solution.py:10
  107.5 70.5 %collective-permute-start.9 = (bf16[320,1280]{1,0:T(8,128)(2,1)S(1)}, bf16[320,1280]{1,0:T(8,128)(2,1)S(1)}, u32[]{:S(2)}, u32[]{:S(2)}) collective-permute-start(bf16[320,1280]{1,0:T(8,128)(2,1)S(1)} %broadcast_select_fusion.16), channel_id=1, source_target_pairs={{0,16},{2,18},{4,20},{6,22},{8,24},{10,26},{12,28},{14,30},{16,0},... | collective-permute-start | bytes 2457608 | tf_op jit(solution)/shard_map/ppermute | solution.py:10
  124.7 69.1 %collective-permute-start.15 = (bf16[320,1280]{1,0:T(8,128)(2,1)S(1)}, bf16[320,1280]{1,0:T(8,128)(2,1)S(1)}, u32[]{:S(2)}, u32[]{:S(2)}) collective-permute-start(bf16[320,1280]{1,0:T(8,128)(2,1)S(1)} %broadcast_select_fusion.9), channel_id=1, source_target_pairs={{0,16},{2,18},{4,20},{6,22},{8,24},{10,26},{12,28},{14,30},{16,0},... | collective-permute-start | bytes 2457608 | tf_op jit(solution)/shard_map/ppermute | solution.py:10
  143.0 53.0 %collective-permute-start.22 = (bf16[320,1280]{1,0:T(8,128)(2,1)S(1)}, bf16[320,1280]{1,0:T(8,128)(2,1)S(1)}, u32[]{:S(2)}, u32[]{:S(2)}) collective-permute-start(bf16[320,1280]{1,0:T(8,128)(2,1)S(1)} %broadcast_select_fusion.3), channel_id=1, source_target_pairs={{0,32},{2,34},{4,36},{6,38},{8,40},{10,42},{12,44},{14,46},{16,48}... | collective-permute-start | bytes 2457608 | tf_op jit(solution)/shard_map/ppermute | solution.py:10
  160.5 38.9 %collective-permute-start.4 = (bf16[320,1280]{1,0:T(8,128)(2,1)S(1)}, bf16[320,1280]{1,0:T(8,128)(2,1)S(1)}, u32[]{:S(2)}, u32[]{:S(2)}) collective-permute-start(bf16[320,1280]{1,0:T(8,128)(2,1)S(1)} %broadcast_select_fusion.24), channel_id=1, source_target_pairs={{0,32},{2,34},{4,36},{6,38},{8,40},{10,42},{12,44},{14,46},{16,48}... | collective-permute-start | bytes 2457608 | tf_op jit(solution)/shard_map/ppermute | solution.py:10
  178.1 21.5 %collective-permute-start.10 = (bf16[320,1280]{1,0:T(8,128)(2,1)S(1)}, bf16[320,1280]{1,0:T(8,128)(2,1)S(1)}, u32[]{:S(2)}, u32[]{:S(2)}) collective-permute-start(bf16[320,1280]{1,0:T(8,128)(2,1)S(1)} %broadcast_select_fusion.17), channel_id=1, source_target_pairs={{0,32},{2,34},{4,36},{6,38},{8,40},{10,42},{12,44},{14,46},{16,48}... | collective-permute-start | bytes 2457608 | tf_op jit(solution)/shard_map/ppermute | solution.py:10
  193.9 36.3 %collective-permute-start.16 = (bf16[320,1280]{1,0:T(8,128)(2,1)S(1)}, bf16[320,1280]{1,0:T(8,128)(2,1)S(1)}, u32[]{:S(2)}, u32[]{:S(2)}) collective-permute-start(bf16[320,1280]{1,0:T(8,128)(2,1)S(1)} %broadcast_select_fusion.10), channel_id=1, source_target_pairs={{0,32},{2,34},{4,36},{6,38},{8,40},{10,42},{12,44},{14,46},{16,48}... | collective-permute-start | bytes 2457608 | tf_op jit(solution)/shard_map/ppermute | solution.py:10
  196.0 110.3 %collective-permute-start.23 = (bf16[320,1280]{1,0:T(8,128)(2,1)S(1)}, bf16[320,1280]{1,0:T(8,128)(2,1)S(1)}, u32[]{:S(2)}, u32[]{:S(2)}) collective-permute-start(bf16[320,1280]{1,0:T(8,128)(2,1)S(1)} %broadcast_select_fusion.4), channel_id=1, source_target_pairs={{0,64},{2,66},{4,68},{6,70},{8,72},{10,74},{12,76},{14,78},{16,80}... | collective-permute-start | bytes 2457608 | tf_op jit(solution)/shard_map/ppermute | solution.py:10
  199.5 133.4 %collective-permute-start.5 = (bf16[320,1280]{1,0:T(8,128)(2,1)S(1)}, bf16[320,1280]{1,0:T(8,128)(2,1)S(1)}, u32[]{:S(2)}, u32[]{:S(2)}) collective-permute-start(bf16[320,1280]{1,0:T(8,128)(2,1)S(1)} %broadcast_select_fusion.25), channel_id=1, source_target_pairs={{0,64},{2,66},{4,68},{6,70},{8,72},{10,74},{12,76},{14,78},{16,80}... | collective-permute-start | bytes 2457608 | tf_op jit(solution)/shard_map/ppermute | solution.py:10
  199.7 168.6 %collective-permute-start.11 = (bf16[320,1280]{1,0:T(8,128)(2,1)S(1)}, bf16[320,1280]{1,0:T(8,128)(2,1)S(1)}, u32[]{:S(2)}, u32[]{:S(2)}) collective-permute-start(bf16[320,1280]{1,0:T(8,128)(2,1)S(1)} %broadcast_select_fusion.18), channel_id=1, source_target_pairs={{0,64},{2,66},{4,68},{6,70},{8,72},{10,74},{12,76},{14,78},{16,80}... | collective-permute-start | bytes 2457608 | tf_op jit(solution)/shard_map/ppermute | solution.py:10
  230.3 170.8 %collective-permute-start.17 = (bf16[320,1280]{1,0:T(8,128)(2,1)S(1)}, bf16[320,1280]{1,0:T(8,128)(2,1)S(1)}, u32[]{:S(2)}, u32[]{:S(2)}) collective-permute-start(bf16[320,1280]{1,0:T(8,128)(2,1)S(1)} %broadcast_select_fusion.11), channel_id=1, source_target_pairs={{0,64},{2,66},{4,68},{6,70},{8,72},{10,74},{12,76},{14,78},{16,80}... | collective-permute-start | bytes 2457608 | tf_op jit(solution)/shard_map/ppermute | solution.py:10
  306.4 178.8 %collective-permute-start.24 = (bf16[320,1280]{1,0:T(8,128)(2,1)S(1)}, bf16[320,1280]{1,0:T(8,128)(2,1)S(1)}, u32[]{:S(2)}, u32[]{:S(2)}) collective-permute-start(bf16[320,1280]{1,0:T(8,128)(2,1)S(1)} %broadcast_select_fusion.5), channel_id=1, source_target_pairs={{0,128},{2,130},{4,132},{6,134},{8,136},{10,138},{12,140},{14,142}... | collective-permute-start | bytes 2457608 | tf_op jit(solution)/shard_map/ppermute | solution.py:10
  333.0 152.3 %collective-permute-start.6 = (bf16[320,1280]{1,0:T(8,128)(2,1)S(1)}, bf16[320,1280]{1,0:T(8,128)(2,1)S(1)}, u32[]{:S(2)}, u32[]{:S(2)}) collective-permute-start(bf16[320,1280]{1,0:T(8,128)(2,1)S(1)} %broadcast_select_fusion.26), channel_id=1, source_target_pairs={{0,128},{2,130},{4,132},{6,134},{8,136},{10,138},{12,140},{14,142}... | collective-permute-start | bytes 2457608 | tf_op jit(solution)/shard_map/ppermute | solution.py:10
  368.4 118.0 %collective-permute-start.12 = (bf16[320,1280]{1,0:T(8,128)(2,1)S(1)}, bf16[320,1280]{1,0:T(8,128)(2,1)S(1)}, u32[]{:S(2)}, u32[]{:S(2)}) collective-permute-start(bf16[320,1280]{1,0:T(8,128)(2,1)S(1)} %broadcast_select_fusion.19), channel_id=1, source_target_pairs={{0,128},{2,130},{4,132},{6,134},{8,136},{10,138},{12,140},{14,142}... | collective-permute-start | bytes 2457608 | tf_op jit(solution)/shard_map/ppermute | solution.py:10
  401.2 103.2 %collective-permute-start.18 = (bf16[320,1280]{1,0:T(8,128)(2,1)S(1)}, bf16[320,1280]{1,0:T(8,128)(2,1)S(1)}, u32[]{:S(2)}, u32[]{:S(2)}) collective-permute-start(bf16[320,1280]{1,0:T(8,128)(2,1)S(1)} %broadcast_select_fusion.12), channel_id=1, source_target_pairs={{0,128},{2,130},{4,132},{6,134},{8,136},{10,138},{12,140},{14,142}... | collective-permute-start | bytes 2457608 | tf_op jit(solution)/shard_map/ppermute | solution.py:10
  485.3 0.9 copy-start.4
  485.4 1.0 copy-start
  486.6 17.9 %copy-start.2 = (bf16[320,1280]{1,0:T(8,128)(2,1)}, bf16[320,1280]{1,0:T(8,128)(2,1)S(1)}, u32[]{:S(2)}) copy-start(bf16[320,1280]{1,0:T(8,128)(2,1)S(1)} %broadcast_select_fusion.20) | copy-start | bytes 2457604
  504.5 3.5 copy-start.6
  504.5 1.2 slice-start.4
  508.2 1.3 slice-start.5
  509.5 384.8 %copy-start.9 = (f32[320,320]{0,1:T(8,128)}, f32[320,320]{0,1:T(8,128)S(1)}, u32[]{:S(2)}) copy-start(f32[320,320]{0,1:T(8,128)S(1)} %get-tuple-element.51) | copy-start | bytes 1228804
  512.2 2.2 slice-start
  517.2 2.2 slice-start.2
  522.2 2.2 slice-start.6
  527.3 2.2 slice-start.1
  531.9 1.3 slice-start.3
  536.0 2.0 slice-start.7
  542.6 353.5 %copy-start.12 = (f32[320,320]{0,1:T(8,128)S(1)}, f32[320,320]{0,1:T(8,128)}, u32[]{:S(2)}) copy-start(f32[320,320]{0,1:T(8,128)} %get-tuple-element.43) | copy-start | bytes 1228804
  542.6 353.5 %copy-start.23 = (f32[320,320]{0,1:T(8,128)S(1)}, f32[320,320]{0,1:T(8,128)}, u32[]{:S(2)}) copy-start(f32[320,320]{0,1:T(8,128)} %get-tuple-element.33) | copy-start | bytes 1228804
  896.1 1.5 copy-start.25
  897.6 2.1 copy-start.14
  897.6 2.2 copy-start.24
  901.3 349.1 %copy-start.5 = (bf16[320,1280]{1,0:T(8,128)(2,1)S(1)}, bf16[320,1280]{1,0:T(8,128)(2,1)}, u32[]{:S(2)}) copy-start(bf16[320,1280]{1,0:T(8,128)(2,1)} %copy-done.4) | copy-start | bytes 2457604
  901.3 349.1 %copy-start.10 = (f32[320,320]{0,1:T(8,128)S(1)}, f32[320,320]{0,1:T(8,128)}, u32[]{:S(2)}) copy-start(f32[320,320]{0,1:T(8,128)} %copy-done.9) | copy-start | bytes 1228804
  1250.4 2.1 copy-start.16
  1250.4 2.1 copy-start.19
  1251.6 1.1 copy-start.7
  1252.8 1.2 copy-start.15
  1252.8 1.2 copy-start.18
  1254.0 1.0 copy-start.13
  1254.0 1.2 copy-start.17
  1255.2 4.0 copy-start.3
  1606.2 1.6 copy-start.1
  1606.3 1.6 copy-start.20
  1606.3 1.7 copy-start.21
  1606.3 1.8 copy-start.22
where the time goes:
time: 1610 us
  blocking collectives  1060 us (66%)
  waiting for transfers between devices  316 us (20%)
  starting transfers between devices  154 us (10%)
  between operations  35.8 us (2%)
  matrix products  27.4 us (2%)
  other arithmetic  16.3 us (1%)
    psum x2, blocking collectives, body(): total_h, total_g = lax.psum((local_h, local_g), 'rows')  687 us
    psum x1, blocking collectives, body(): total_s, total_t = lax.psum((total_s, total_t), 'rows')  344 us
    ppermute x25, waiting for transfers between devices, swapped_2(): return lax.ppermute(value, axis, pairs)  316 us
    ppermute x25, starting transfers between devices, swapped_2(): return lax.ppermute(value, axis, pairs)  154 us
  transfers between devices with their start and end apart: 25, of which 15 were waited for; matrix products, arithmetic and copies ran while one was open for 0% of the time, Pallas kernels for 0%

commit v1 on v0

v1 whole, which is shorter than its diff:
```python
import functools
import jax
import jax.numpy as jnp
from jax import lax
from jax.experimental import pallas as pl
from jax.experimental.pallas import tpu as pltpu
from jax.sharding import PartitionSpec as P

MESH = pl.DeviceIdType.MESH
F32 = jnp.float32
BF16 = jnp.bfloat16
NZ = 8
NP = 16
ROWS = 320
HALF = 160
CR = 80
CC = 128
ROUNDS = 4
TILES = ROUNDS + 1
SQ = 512
UQ = 256


def nt_dot(a, b):
    return lax.dot_general(a, b, (((1,), (1,)), ((), ())), preferred_element_type=F32)


def col_norms(m):
    x = m.astype(F32)
    sq = x * x
    hi = sq.astype(BF16)
    lo = (sq - hi.astype(F32)).astype(BF16)
    ones = jnp.ones((8, m.shape[1]), BF16)
    return (nt_dot(ones, hi) + nt_dot(ones, lo))[0:1, :]


def row_norms(m):
    x = m.astype(F32)
    return jnp.sum(x * x, axis=1, keepdims=True)


def wait_bytes(ref, sem):
    pltpu.make_async_copy(ref, ref, sem).wait()


def kernel(pairs, rounds_ref, s_ref, t_ref, grad_ref, loss_ref,
           gs, gt, gu, stage_s, stage_t, stage_u, ms, mt, mu,
           rn_s, rn_t, ds, dt, xs, xt, ys, yt, wb, rsum, pv, pa, pb,
           p1_send, p1_recv, ring_send, ring_recv, p2_send, p2_recv,
           x_send, x_recv, w_send, w_recv, r_send, r_recv, ps_send, ps_recv):
    row = lax.axis_index("rows")
    core = lax.axis_index("feat")
    z = row // NP
    me = row % NP
    other = 1 - core
    holder = (me // 8) == core
    base = z * NP

    def plane(d):
        return {"rows": base + d}

    def line(q):
        return {"rows": (q % NZ) * NP + me, "feat": q // NZ}

    q_me = core * NZ + z
    right = {"rows": ((z + 1) % NZ) * NP + me}
    left = {"rows": ((z + NZ - 1) % NZ) * NP + me}
    mate_core = {"feat": other}

    barrier = pltpu.get_barrier_semaphore()

    def greet(k, carry):
        pl.semaphore_signal(barrier, inc=1, device_id=plane((me + k) % NP), device_id_type=MESH)
        pl.semaphore_signal(barrier, inc=1, device_id=line((q_me + k) % NP), device_id_type=MESH)
        return carry
    lax.fori_loop(1, NP, greet, 0)
    pl.semaphore_wait(barrier, 2 * (NP - 1))

    def rect(ref, i, first=0):
        r0 = pl.multiple_of((i % 4) * CR, 16)
        c0 = pl.multiple_of(first + (i // 4) * CC, CC)
        return ref.at[pl.ds(r0, CR), pl.ds(c0, CC)]

    def scatter(src, g, slot):
        def one(k, carry):
            d = (me + k) % NP
            pltpu.make_async_remote_copy(
                rect(src, d), g.at[z, me], p1_send.at[slot], p1_recv.at[slot],
                device_id=plane(d), device_id_type=MESH).start()
            return carry
        lax.fori_loop(1, NP, one, 0)
        pltpu.make_async_copy(rect(src, me), g.at[z, me], p1_recv.at[slot]).start()

    def scatter_u():
        def one(j, carry):
            d = core * 8 + j

            @pl.when(d != me)
            def _():
                pltpu.make_async_remote_copy(
                    rect(t_ref, j, SQ), gu.at[z, me], p1_send.at[2], p1_recv.at[2],
                    device_id=plane(d), device_id_type=MESH).start()
            return carry
        lax.fori_loop(0, 8, one, 0)

        @pl.when(holder)
        def _():
            pltpu.make_async_copy(rect(t_ref, me % 8, SQ), gu.at[z, me], p1_recv.at[2]).start()

    def ring_pair(g, slot, step):
        br = (z + NZ - step) % NZ
        bl = (z + step) % NZ
        r_ref, l_ref = g.at[br], g.at[bl]
        if step == NZ // 2 - 1:
            r_ref = r_ref.at[pl.ds(0, NP // 2)]
            l_ref = l_ref.at[pl.ds(NP // 2, NP // 2)]
        a = pltpu.make_async_remote_copy(
            r_ref, r_ref, ring_send.at[slot, 0, step], ring_recv.at[slot, 0, step],
            device_id=right, device_id_type=MESH)
        b = pltpu.make_async_remote_copy(
            l_ref, l_ref, ring_send.at[slot, 1, step], ring_recv.at[slot, 1, step],
            device_id=left, device_id_type=MESH)
        return a, b

    def ring_start(g, slot, step):
        if step > 0:
            a, b = ring_pair(g, slot, step - 1)
            a.wait_recv()
            b.wait_recv()
        if step < NZ // 2:
            a, b = ring_pair(g, slot, step)
            a.start()
            b.start()

    def ring_flush(g, slot):
        for step in range(NZ // 2):
            a, b = ring_pair(g, slot, step)
            a.wait_send()
            b.wait_send()

    def deliver(g, stage, mate, slot, r, i):
        mask = rounds_ref[r]
        zz = z ^ (mask // NP)
        low = mask % NP

        def one(d, carry):
            stage[r, d] = g[zz, d ^ low]

            @pl.when(d != me)
            def _():
                pltpu.make_async_remote_copy(
                    stage.at[r, d], rect(mate.at[r], i), p2_send.at[slot, r], p2_recv.at[slot, r],
                    device_id=plane(d), device_id_type=MESH).start()

            @pl.when(d == me)
            def _():
                pltpu.make_async_copy(stage.at[r, d], rect(mate.at[r], i), p2_recv.at[slot, r]).start()
            return carry
        lax.fori_loop(0, NP, one, 0)

    own_rows = pl.ds(pl.multiple_of(core * HALF, 16), HALF)
    far_rows = pl.ds(pl.multiple_of(other * HALF, 16), HALF)

    def cross(x, y, side, k):
        return pltpu.make_async_remote_copy(
            x.at[k], y.at[k], x_send.at[side, k], x_recv.at[side, k],
            device_id=mate_core, device_id_type=MESH)

    def tile_s(k, m):
        cn = col_norms(m)
        xs[k] = rn_s[far_rows, 0:1] + cn - 2.0 * nt_dot(s_ref[far_rows, :], m)
        cross(xs, ys, 0, k).start()
        ds[k] = rn_s[own_rows, 0:1] + cn - 2.0 * nt_dot(s_ref[own_rows, :], m)

    def tile_t(k, m):
        cn = col_norms(m)
        xt[k] = rn_t[far_rows, 0:1] + cn - 2.0 * nt_dot(t_ref[far_rows, 0:SQ], m)
        dt[k] = rn_t[own_rows, 0:1] + cn - 2.0 * nt_dot(t_ref[own_rows, 0:SQ], m)

    def tile_u(k, m):
        cn = col_norms(m)
        xt[k] += cn - 2.0 * nt_dot(t_ref[far_rows, SQ:SQ + UQ], m)
        cross(xt, yt, 1, k).start()
        dt[k] += cn - 2.0 * nt_dot(t_ref[own_rows, SQ:SQ + UQ], m)

    def finish(d, x, y, side):
        def one(k, acc):
            cross(x, y, side, k).wait_recv()
            v = jnp.sqrt(d[k] + y[k] + 1.0)
            d[k] = v
            return acc + jnp.sum(v, axis=0, keepdims=True)
        acc = lax.fori_loop(0, TILES, one, jnp.zeros((1, ROWS), F32))
        return jnp.sum(acc, axis=1, keepdims=True)

    def all_sum(n, a, b):
        first = lax.broadcasted_iota(jnp.int32, (8, 128), 0) == 0
        v = jnp.where(first, a, b)
        pv[n, 0] = v
        pa[n, me] = v

        def send_a(k, carry):
            pltpu.make_async_remote_copy(
                pv.at[n, 0], pa.at[n, me], ps_send.at[n, 0], ps_recv.at[n, 0],
                device_id=plane((me + k) % NP), device_id_type=MESH).start()
            return carry
        lax.fori_loop(1, NP, send_a, 0)
        wait_bytes(pa.at[n, pl.ds(0, NP - 1)], ps_recv.at[n, 0])
        v = jnp.sum(pa[n], axis=0)
        pv[n, 1] = v
        pb[n, q_me] = v

        def send_b(k, carry):
            pltpu.make_async_remote_copy(
                pv.at[n, 1], pb.at[n, q_me], ps_send.at[n, 1], ps_recv.at[n, 1],
                device_id=line((q_me + k) % NP), device_id_type=MESH).start()
            return carry
        lax.fori_loop(1, NP, send_b, 0)
        wait_bytes(pb.at[n, pl.ds(0, NP - 1)], ps_recv.at[n, 1])
        v = jnp.sum(pb[n], axis=0)
        return v[0:1, 0:1], v[1:2, 0:1]

    scatter(s_ref, gs, 0)
    rn_s[...] = jnp.broadcast_to(row_norms(s_ref[...]), (ROWS, 128))
    wait_bytes(gs.at[z], p1_recv.at[0])
    ring_start(gs, 0, 0)
    scatter(t_ref, gt, 1)
    scatter_u()
    rn_t[...] = jnp.broadcast_to(row_norms(t_ref[...]), (ROWS, 128))
    wait_bytes(gt.at[z], p1_recv.at[1])
    ring_start(gt, 1, 0)
    tile_s(0, s_ref[...])
    ring_start(gs, 0, 1)
    tile_t(0, t_ref[:, 0:SQ])
    ring_start(gs, 0, 2)
    tile_u(0, t_ref[:, SQ:SQ + UQ])
    ring_start(gs, 0, 3)

    ring_start(gt, 1, 1)

    @pl.when(holder)
    def _():
        wait_bytes(gu.at[z], p1_recv.at[2])
        ring_start(gu, 2, 0)
    ring_start(gs, 0, 4)
    deliver(gs, stage_s, ms, 0, 0, me)
    deliver(gs, stage_s, ms, 0, 1, me)
    ring_start(gt, 1, 2)
    deliver(gs, stage_s, ms, 0, 2, me)
    deliver(gs, stage_s, ms, 0, 3, me)
    ring_start(gt, 1, 3)

    @pl.when(holder)
    def _():
        ring_start(gu, 2, 1)

    def mate_s(r, carry):
        wait_bytes(ms.at[r], p2_recv.at[0, r])
        tile_s(r + 1, ms[r])
        return carry
    lax.fori_loop(0, 2, mate_s, 0)

    @pl.when(holder)
    def _():
        ring_start(gu, 2, 2)
    ring_start(gt, 1, 4)
    for r in range(ROUNDS):
        deliver(gt, stage_t, mt, 1, r, me)

    @pl.when(holder)
    def _():
        ring_start(gu, 2, 3)
    lax.fori_loop(2, ROUNDS, mate_s, 0)

    @pl.when(holder)
    def _():
        ring_start(gu, 2, 4)
        for r in range(ROUNDS):
            deliver(gu, stage_u, mu, 2, r, me % 8)

    sum_s = finish(ds, xs, ys, 0)

    def mate_t(r, carry):
        wait_bytes(mt.at[r], p2_recv.at[1, r])
        tile_t(r + 1, mt[r])
        return carry
    lax.fori_loop(0, ROUNDS, mate_t, 0)

    def mate_u(r, carry):
        wait_bytes(mu.at[r], p2_recv.at[2, r])
        tile_u(r + 1, mu[r])
        return carry
    lax.fori_loop(0, ROUNDS, mate_u, 0)
    sum_t = finish(dt, xt, yt, 1)

    total_s, total_t = all_sum(0, sum_s, sum_t)
    mean_s = total_s / pairs
    mean_t = total_t / pairs
    inv_s = 1.0 / mean_s
    inv_t = 1.0 / mean_t

    def second(k, carry):
        h, g = carry
        d = ds[k]
        err = d * inv_s - dt[k] * inv_t
        size = jnp.abs(err)
        slope = jnp.clip(err, -1.0, 1.0)
        hub = jnp.where(size < 1.0, 0.5 * err * err, size - 0.5)
        dt[k] = slope
        return (h + jnp.sum(hub, axis=0, keepdims=True),
                g + jnp.sum(slope * d, axis=0, keepdims=True))
    zero = jnp.zeros((1, ROWS), F32)
    acc_h, acc_g = lax.fori_loop(0, TILES, second, (zero, zero))
    total_h, total_g = all_sum(
        1, jnp.sum(acc_h, axis=1, keepdims=True), jnp.sum(acc_g, axis=1, keepdims=True))
    loss_ref[...] = jnp.broadcast_to(total_h / pairs, (8, 128))
    kappa = total_g / (mean_s * pairs)

    def weights_copy(k):
        part = wb.at[k, own_rows]
        return pltpu.make_async_remote_copy(
            part, part, w_send.at[k], w_recv.at[k], device_id=mate_core, device_id_type=MESH)

    def third(k, acc):
        w = (dt[k] - kappa) / ds[k]
        wb[k, own_rows] = w.astype(BF16)
        weights_copy(k).start()
        return acc + jnp.sum(w, axis=1, keepdims=True)
    sums = lax.fori_loop(0, TILES, third, jnp.zeros((HALF, 1), F32))
    rsum[own_rows, :] = jnp.broadcast_to(sums, (HALF, 128))
    sums_copy = pltpu.make_async_remote_copy(
        rsum.at[own_rows], rsum.at[own_rows], r_send, r_recv,
        device_id=mate_core, device_id_type=MESH)
    sums_copy.start()

    weights_copy(0).wait_recv()
    grad_ref[...] = jnp.dot(wb[0], s_ref[...], preferred_element_type=F32)

    def pull(r, carry):
        weights_copy(r + 1).wait_recv()
        grad_ref[...] += jnp.dot(wb[r + 1], ms[r], preferred_element_type=F32)
        return carry
    lax.fori_loop(0, ROUNDS, pull, 0)
    sums_copy.wait_recv()
    grad_ref[...] = 2.0 * (rsum[:, 0:1] * s_ref[...].astype(F32) - grad_ref[...])

    wait_bytes(gs.at[0, pl.ds(0, NP - 1)], p1_send.at[0])
    wait_bytes(gt.at[0, pl.ds(0, NP - 1)], p1_send.at[1])
    ring_flush(gs, 0)
    ring_flush(gt, 1)

    @pl.when(holder)
    def _():
        wait_bytes(gu.at[0, pl.ds(0, 7)], p1_send.at[2])
        ring_flush(gu, 2)
        for r in range(ROUNDS):
            wait_bytes(stage_u.at[r, pl.ds(0, NP - 1)], p2_send.at[2, r])

    @pl.when(jnp.logical_not(holder))
    def _():
        wait_bytes(gu.at[0, pl.ds(0, 8)], p1_send.at[2])
    for r in range(ROUNDS):
        wait_bytes(stage_s.at[r, pl.ds(0, NP - 1)], p2_send.at[0, r])
        wait_bytes(stage_t.at[r, pl.ds(0, NP - 1)], p2_send.at[1, r])
    for k in range(TILES):
        cross(xs, ys, 0, k).wait_send()
        cross(xt, yt, 1, k).wait_send()
        weights_copy(k).wait_send()
    sums_copy.wait_send()
    for n in range(2):
        for half in range(2):
            wait_bytes(pa.at[n, pl.ds(0, NP - 1)], ps_send.at[n, half])


def body(student, teacher, rounds):
    pairs = float(NZ * NP * TILES * ROWS * ROWS)
    vmem = pl.BlockSpec(memory_space=pltpu.VMEM)
    dma = pltpu.SemaphoreType.DMA
    grad, loss = pl.pallas_call(
        functools.partial(kernel, pairs),
        out_shape=(jax.ShapeDtypeStruct((ROWS, SQ), F32), jax.ShapeDtypeStruct((8, 128), F32)),
        in_specs=[pl.BlockSpec(memory_space=pltpu.SMEM), vmem, vmem],
        out_specs=(vmem, vmem),
        scratch_shapes=[
            pltpu.VMEM((NZ, NP, CR, CC), BF16),
            pltpu.VMEM((NZ, NP, CR, CC), BF16),
            pltpu.VMEM((NZ, NP, CR, CC), BF16),
            pltpu.VMEM((ROUNDS, NP, CR, CC), BF16),
            pltpu.VMEM((ROUNDS, NP, CR, CC), BF16),
            pltpu.VMEM((ROUNDS, NP, CR, CC), BF16),
            pltpu.VMEM((ROUNDS, ROWS, SQ), BF16),
            pltpu.VMEM((ROUNDS, ROWS, SQ), BF16),
            pltpu.VMEM((ROUNDS, ROWS, UQ), BF16),
            pltpu.VMEM((ROWS, 128), F32),
            pltpu.VMEM((ROWS, 128), F32),
            pltpu.VMEM((TILES, HALF, ROWS), F32),
            pltpu.VMEM((TILES, HALF, ROWS), F32),
            pltpu.VMEM((TILES, HALF, ROWS), F32),
            pltpu.VMEM((TILES, HALF, ROWS), F32),
            pltpu.VMEM((TILES, HALF, ROWS), F32),
            pltpu.VMEM((TILES, HALF, ROWS), F32),
            pltpu.VMEM((TILES, ROWS, ROWS), BF16),
            pltpu.VMEM((ROWS, 128), F32),
            pltpu.VMEM((2, 2, 8, 128), F32),
            pltpu.VMEM((2, NP, 8, 128), F32),
            pltpu.VMEM((2, NP, 8, 128), F32),
            dma((3,)), dma((3,)),
            dma((3, 2, NZ // 2)), dma((3, 2, NZ // 2)),
            dma((3, ROUNDS)), dma((3, ROUNDS)),
            dma((2, TILES)), dma((2, TILES)),
            dma((TILES,)), dma((TILES,)),
            dma, dma,
            dma((2, 2)), dma((2, 2)),
        ],
        compiler_params=pltpu.CompilerParams(
            collective_id=0, has_side_effects=True, vmem_limit_bytes=56 * 1024 * 1024),
        name="relation",
    )(rounds, student, teacher)
    return grad, loss[0, 0]


def solution(mesh):
    return jax.shard_map(
        body,
        mesh=mesh,
        in_specs=(P("rows", "feat"), P("rows", "feat"), P()),
        out_specs=(P("rows", "feat"), P()),
        check_vma=False,
    )
```

time: 1610 us -> 133 us (0.08)
  blocking collectives: 1060 us -> 0 us
  waiting for transfers between devices: 316 us -> 0 us
  starting transfers between devices: 154 us -> 0 us
  Pallas kernels: 0 us -> 127 us
  between operations: 35.8 us -> 0.64 us
  matrix products: 27.4 us -> 0 us
  other arithmetic: 16.3 us -> 0 us
    psum x3 -> x0, blocking collectives: 1030 us -> none  [the longest x2 687 us: body(): total_h, total_g = lax.psum((local_h, local_g), 'rows')]
    ppermute x25 -> x0, waiting for transfers between devices: 316 us -> none  [swapped_2(): return lax.ppermute(value, axis, pairs)]
    ppermute x25 -> x0, starting transfers between devices: 154 us -> none  [swapped_2(): return lax.ppermute(value, axis, pairs)]
    pallas_call x0 -> x1, Pallas kernels: none -> 127 us  [body(): pl.pallas_call(functools.partial(kernel, pairs), out_shape=(jax.ShapeDtyp...]
    dot_general x15 -> x0, matrix products: 27.4 us -> none  [the longest x5 11 us: body(): inner_t = jnp.dot(full_own_t, wide_t.T, preferred_element_type=jnp.float32)]
    all_gather x10 -> x0, blocking collectives: 24 us -> none  [the longest x5 12.5 us: body(): lax.all_gather(mate_t, 'feat', axis=1, tiled=True)]
  transfers between devices with their start and end apart: 25 -> 0, of which waited for: 15 -> 0; matrix products, arithmetic and copies ran while one was open for 0% -> 0% of each run, Pallas kernels for 0% -> 0%
where the time goes in v1:
time: 133 us; the launch traced here: 131 us
  Pallas kernels  127 us (95%)
  local copies, waits for them, and re-layouts  3.16 us (2%)
    pallas_call x1, Pallas kernels, body(): pl.pallas_call(functools.partial(kernel, pairs), out_shape=(jax.ShapeDtyp...  127 us

profile of v1, /device:TPU:2, one launch (start us, length us, event | category | flops | bytes accessed | tf_op | source)
XLA Modules:
  0.0 130.8 jit_solution(12629366434844985353)
XLA Ops:
  0.6 127.0 %relation.1 = (f32[320,512]{1,0:T(8,128)}, f32[8,128]{1,0:T(8,128)}) custom-call(s32[4]{0:T(128)} %rounds_ref.1, bf16[320,512]{1,0:T(8,128)(2,1)} %s_ref.1, bf16[320,768]{1,0:T(8,128)(2,1)} %t_ref.1), custom_call_target="tpu_custom_call" | custom-call | tf_op jit(solution)/shard_map/relation/pallas_call | solution.py:378
  127.6 1.2 slice.3
  128.8 2.0 %copy.6 = f32[320,512]{1,0:T(8,128)} copy(f32[320,512]{1,0:T(8,128)} %get-tuple-element.8) | data formatting | bytes 1310720

commit v2 on v1

v2 whole, which is shorter than its diff:
```python
import functools
import jax
import jax.numpy as jnp
from jax import lax
from jax.experimental import pallas as pl
from jax.experimental.pallas import tpu as pltpu
from jax.sharding import PartitionSpec as P

MESH = pl.DeviceIdType.MESH
F32 = jnp.float32
BF16 = jnp.bfloat16
NZ = 8
NP = 16
ROWS = 320
HALF = 160
CR = 80
CC = 128
ROUNDS = 4
TILES = ROUNDS + 1
SQ = 512
UQ = 256
VA = 48
VB = 32
PARTS = 4


def nt_dot(a, b):
    return lax.dot_general(a, b, (((1,), (1,)), ((), ())), preferred_element_type=F32)


def col_norms(m):
    x = m.astype(F32)
    sq = x * x
    hi = sq.astype(BF16)
    lo = (sq - hi.astype(F32)).astype(BF16)
    ones = jnp.ones((8, m.shape[1]), BF16)
    return (nt_dot(ones, hi) + nt_dot(ones, lo))[0:1, :]


def row_norms(m):
    x = m.astype(F32)
    return jnp.sum(x * x, axis=1, keepdims=True)


def wait_bytes(ref, sem):
    pltpu.make_async_copy(ref, ref, sem).wait()


def kernel(pairs, rounds_ref, s_hbm, t_hbm, ga_ref, gb_ref, scal_ref,
           s_ref, t_ref, gs, gu, ga, gb, stage_s, stage_u, stage_a, stage_b, ms, mt, mu,
           rn_s, rn_t, ds, dt, xs, xt, ys, yt, wa, wb, ra, rb, pv, pa, pb,
           in_sem, p1_send, p1_recv, ring_send, ring_recv, p2_send, p2_recv,
           x_send, x_recv, w_send, w_recv, r_send, r_recv, ps_send, ps_recv):
    load_s = pltpu.make_async_copy(s_hbm, s_ref, in_sem.at[0])
    load_t = pltpu.make_async_copy(t_hbm, t_ref, in_sem.at[1])
    load_s.start()
    load_t.start()
    row = lax.axis_index("rows")
    core = lax.axis_index("feat")
    z = row // NP
    me = row % NP
    other = 1 - core
    holder = (me // 8) == core
    base = z * NP

    def plane(d):
        return {"rows": base + d}

    def line(q):
        return {"rows": (q % NZ) * NP + me, "feat": q // NZ}

    q_me = core * NZ + z
    right = {"rows": ((z + 1) % NZ) * NP + me}
    left = {"rows": ((z + NZ - 1) % NZ) * NP + me}
    mate_core = {"feat": other}

    barrier = pltpu.get_barrier_semaphore()

    def greet(k, carry):
        pl.semaphore_signal(barrier, inc=1, device_id=plane((me + k) % NP), device_id_type=MESH)
        pl.semaphore_signal(barrier, inc=1, device_id=line((q_me + k) % NP), device_id_type=MESH)
        return carry
    lax.fori_loop(1, NP, greet, 0)
    load_s.wait()
    rn_s[...] = jnp.broadcast_to(row_norms(s_ref[...]), (ROWS, 128))
    load_t.wait()
    rn_t[...] = jnp.broadcast_to(row_norms(t_ref[...]), (ROWS, 128))
    pl.semaphore_wait(barrier, 2 * (NP - 1))

    S, U, A, B = (0, 0, 0, CR), (1, SQ, 0, CR), (2, 0, 0, VA), (3, 0, VA, VB)

    def rect(ref, i, piece, first=0):
        r0 = pl.multiple_of((i % 4) * CR + piece[2], 16)
        c0 = pl.multiple_of(first + (i // 4) * CC, CC)
        return ref.at[pl.ds(r0, piece[3]), pl.ds(c0, CC)]

    def scatter(src, g, piece):
        slot = piece[0]

        def one(k, carry):
            d = (me + k) % NP
            pltpu.make_async_remote_copy(
                rect(src, d, piece), g.at[z, me], p1_send.at[slot], p1_recv.at[slot],
                device_id=plane(d), device_id_type=MESH).start()
            return carry
        lax.fori_loop(1, NP, one, 0)
        pltpu.make_async_copy(rect(src, me, piece), g.at[z, me], p1_recv.at[slot]).start()

    def scatter_u():
        def one(j, carry):
            d = core * 8 + j

            @pl.when(d != me)
            def _():
                pltpu.make_async_remote_copy(
                    rect(t_ref, j, U, SQ), gu.at[z, me], p1_send.at[1], p1_recv.at[1],
                    device_id=plane(d), device_id_type=MESH).start()
            return carry
        lax.fori_loop(0, 8, one, 0)

        @pl.when(holder)
        def _():
            pltpu.make_async_copy(rect(t_ref, me % 8, U, SQ), gu.at[z, me], p1_recv.at[1]).start()

    def scattered(g, piece):
        wait_bytes(g.at[z], p1_recv.at[piece[0]])

    def ring_copy(g, slot, way, part, step):
        block = (z + NZ - step) % NZ if way == 0 else (z + step) % NZ
        ref = g.at[block, pl.ds(part * (NP // PARTS), NP // PARTS)]
        return pltpu.make_async_remote_copy(
            ref, ref, ring_send.at[slot, way, part, step], ring_recv.at[slot, way, part, step],
            device_id=right if way == 0 else left, device_id_type=MESH)

    def ways(part, step):
        return (0, 1) if step < NZ // 2 - 1 else (part // (PARTS // 2),)

    def ring(g, piece, step, parts=range(PARTS)):
        slot = piece[0]
        for part in parts:
            if step > 0:
                for way in ways(part, step - 1):
                    ring_copy(g, slot, way, part, step - 1).wait_recv()
            if step < NZ // 2:
                for way in ways(part, step):
                    ring_copy(g, slot, way, part, step).start()

    def ring_flush(g, piece):
        for step in range(NZ // 2):
            for part in range(PARTS):
                for way in ways(part, step):
                    ring_copy(g, piece[0], way, part, step).wait_send()

    def ring_u(step):
        @pl.when(holder)
        def _():
            if step == 0:
                scattered(gu, U)
            ring(gu, U, step)

    def deliver(g, stage, mate, piece, r, i):
        slot = piece[0]
        mask = rounds_ref[r]
        zz = z ^ (mask // NP)
        low = mask % NP

        def one(d, carry):
            stage[r, d] = g[zz, d ^ low]

            @pl.when(d != me)
            def _():
                pltpu.make_async_remote_copy(
                    stage.at[r, d], rect(mate.at[r], i, piece), p2_send.at[slot, r], p2_recv.at[slot, r],
                    device_id=plane(d), device_id_type=MESH).start()

            @pl.when(d == me)
            def _():
                pltpu.make_async_copy(stage.at[r, d], rect(mate.at[r], i, piece), p2_recv.at[slot, r]).start()
            return carry
        lax.fori_loop(0, NP, one, 0)

    own_rows = pl.ds(pl.multiple_of(core * HALF, 16), HALF)
    far_rows = pl.ds(pl.multiple_of(other * HALF, 16), HALF)

    def cross(x, y, side, k):
        return pltpu.make_async_remote_copy(
            x.at[k], y.at[k], x_send.at[side, k], x_recv.at[side, k],
            device_id=mate_core, device_id_type=MESH)

    def tile_s(k, m):
        cn = col_norms(m)
        xs[k] = rn_s[far_rows, 0:1] + cn - 2.0 * nt_dot(s_ref[far_rows, :], m)
        cross(xs, ys, 0, k).start()
        ds[k] = rn_s[own_rows, 0:1] + cn - 2.0 * nt_dot(s_ref[own_rows, :], m)

    def tile_u(k, m):
        cn = col_norms(m)
        xt[k] = rn_t[far_rows, 0:1] + cn - 2.0 * nt_dot(t_ref[far_rows, SQ:SQ + UQ], m)
        dt[k] = rn_t[own_rows, 0:1] + cn - 2.0 * nt_dot(t_ref[own_rows, SQ:SQ + UQ], m)

    def tile_t(k, m):
        cn = col_norms(m)
        xt[k] += cn - 2.0 * nt_dot(t_ref[far_rows, 0:SQ], m)
        cross(xt, yt, 1, k).start()
        dt[k] += cn - 2.0 * nt_dot(t_ref[own_rows, 0:SQ], m)

    def finish(d, x, y, side):
        def one(k, acc):
            cross(x, y, side, k).wait_recv()
            v = jnp.sqrt(d[k] + y[k] + 1.0)
            d[k] = v
            return acc + jnp.sum(v, axis=0, keepdims=True)
        acc = lax.fori_loop(0, TILES, one, jnp.zeros((1, ROWS), F32))
        return jnp.sum(acc, axis=1, keepdims=True)

    def sum_first(n, a, b):
        first = lax.broadcasted_iota(jnp.int32, (8, 128), 0) == 0
        v = jnp.where(first, a, b)
        pv[n, 0] = v
        pa[n, me] = v

        def send(k, carry):
            pltpu.make_async_remote_copy(
                pv.at[n, 0], pa.at[n, me], ps_send.at[n, 0], ps_recv.at[n, 0],
                device_id=plane((me + k) % NP), device_id_type=MESH).start()
            return carry
        lax.fori_loop(1, NP, send, 0)

    def sum_second(n):
        wait_bytes(pa.at[n, pl.ds(0, NP - 1)], ps_recv.at[n, 0])
        v = jnp.sum(pa[n], axis=0)
        pv[n, 1] = v
        pb[n, q_me] = v

        def send(k, carry):
            pltpu.make_async_remote_copy(
                pv.at[n, 1], pb.at[n, q_me], ps_send.at[n, 1], ps_recv.at[n, 1],
                device_id=line((q_me + k) % NP), device_id_type=MESH).start()
            return carry
        lax.fori_loop(1, NP, send, 0)

    def sum_result(n):
        wait_bytes(pb.at[n, pl.ds(0, NP - 1)], ps_recv.at[n, 1])
        v = jnp.sum(pb[n], axis=0)
        return v[0:1, 0:1], v[1:2, 0:1]

    def weights_copy(w, side, k):
        part = w.at[k, own_rows]
        return pltpu.make_async_remote_copy(
            part, part, w_send.at[side, k], w_recv.at[side, k],
            device_id=mate_core, device_id_type=MESH)

    def sums_copy(r, side):
        part = r.at[own_rows]
        return pltpu.make_async_remote_copy(
            part, part, r_send.at[side], r_recv.at[side],
            device_id=mate_core, device_id_type=MESH)

    def send_sums(r, side, sums):
        r[own_rows, :] = jnp.broadcast_to(sums, (HALF, 128))
        sums_copy(r, side).start()

    def pull(w, side, r, g_ref):
        weights_copy(w, side, 0).wait_recv()
        sums_copy(r, side).wait_recv()
        g_ref[...] = (r[:, 0:1] * s_ref[...].astype(F32)
                      - jnp.dot(w[0], s_ref[...], preferred_element_type=F32))

        def one(k, carry):
            weights_copy(w, side, k + 1).wait_recv()
            g_ref[...] -= jnp.dot(w[k + 1], ms[k], preferred_element_type=F32)
            return carry
        lax.fori_loop(0, ROUNDS, one, 0)

    def mate_s(r, carry):
        wait_bytes(stage_s.at[r], p2_recv.at[S[0], r])
        tile_s(r + 1, ms[r])
        return carry

    def mate_u(r, carry):
        wait_bytes(mu.at[r], p2_recv.at[U[0], r])
        tile_u(r + 1, mu[r])
        return carry

    def mate_t(r, carry):
        wait_bytes(stage_a.at[r], p2_recv.at[A[0], r])
        wait_bytes(stage_b.at[r], p2_recv.at[B[0], r])
        tile_t(r + 1, mt[r])
        return carry

    def inverse(k, acc):
        v = 1.0 / ds[k]
        xs[k] = v
        wb[k, own_rows] = v.astype(BF16)
        weights_copy(wb, 1, k).start()
        return acc + jnp.sum(v, axis=1, keepdims=True)

    def deliver_u(*turns):
        @pl.when(holder)
        def _():
            for r in turns:
                deliver(gu, stage_u, mu, U, r, me % 8)

    def deliver_s(r):
        deliver(gs, stage_s, ms, S, r, me)

    def deliver_a(r):
        deliver(ga, stage_a, mt, A, r, me)

    def deliver_b(r):
        deliver(gb, stage_b, mt, B, r, me)

    scatter(s_ref, gs, S)
    scattered(gs, S)
    ring(gs, S, 0)
    scatter_u()
    scatter(t_ref, ga, A)
    scatter(t_ref, gb, B)
    tile_s(0, s_ref[...])
    ring(gs, S, 1)
    tile_u(0, t_ref[:, SQ:SQ + UQ])
    tile_t(0, t_ref[:, 0:SQ])
    ring(gs, S, 2)
    ring_u(0)
    ring(gs, S, 3)
    scattered(ga, A)
    ring(ga, A, 0)
    ring_u(1)
    ring(gs, S, 4)
    deliver_s(0)
    ring(ga, A, 1)
    deliver_s(1)
    ring_u(2)
    deliver_s(2)
    ring(ga, A, 2)
    deliver_s(3)
    ring_u(3)
    ring(ga, A, 3)
    scattered(gb, B)
    ring(gb, B, 0)
    ring_u(4)
    deliver_u(0)
    deliver_u(1)
    ring(ga, A, 4)
    deliver_u(2)
    ring(gb, B, 1)
    deliver_u(3)
    deliver_a(0)
    ring(gb, B, 2)
    deliver_a(1)
    deliver_a(2)
    ring(gb, B, 3)
    deliver_a(3)
    lax.fori_loop(0, ROUNDS, mate_s, 0)
    ring(gb, B, 4)
    for r in range(ROUNDS):
        deliver_b(r)
    lax.fori_loop(0, ROUNDS, mate_u, 0)
    sum_s = finish(ds, xs, ys, 0)
    for k in range(TILES):
        cross(xs, ys, 0, k).wait_send()
    send_sums(rb, 1, lax.fori_loop(0, TILES, inverse, jnp.zeros((HALF, 1), F32)))
    pull(wb, 1, rb, gb_ref)
    lax.fori_loop(0, ROUNDS, mate_t, 0)
    sum_t = finish(dt, xt, yt, 1)

    sum_first(0, sum_s, sum_t)
    sum_second(0)
    total_s, total_t = sum_result(0)
    mean_s = total_s / pairs
    inv_s = 1.0 / mean_s
    inv_t = pairs / total_t

    def second(k, carry):
        h, g, acc = carry
        d = ds[k]
        err = d * inv_s - dt[k] * inv_t
        size = jnp.abs(err)
        slope = jnp.clip(err, -1.0, 1.0)
        hub = jnp.where(size < 1.0, 0.5 * err * err, size - 0.5)
        w = slope * xs[k]
        wa[k, own_rows] = w.astype(BF16)
        weights_copy(wa, 0, k).start()
        return (h + jnp.sum(hub, axis=0, keepdims=True),
                g + jnp.sum(slope * d, axis=0, keepdims=True),
                acc + jnp.sum(w, axis=1, keepdims=True))
    zero = jnp.zeros((1, ROWS), F32)
    acc_h, acc_g, sums = lax.fori_loop(0, TILES, second, (zero, zero, jnp.zeros((HALF, 1), F32)))
    sum_first(1, jnp.sum(acc_h, axis=1, keepdims=True), jnp.sum(acc_g, axis=1, keepdims=True))
    send_sums(ra, 0, sums)
    sum_second(1)
    pull(wa, 0, ra, ga_ref)
    total_h, total_g = sum_result(1)
    first = lax.broadcasted_iota(jnp.int32, (8, 128), 0) == 0
    scal_ref[...] = jnp.where(first, total_g / (mean_s * pairs), total_h / pairs)

    for g, piece, stage in ((gs, S, stage_s), (ga, A, stage_a), (gb, B, stage_b)):
        wait_bytes(g.at[0, pl.ds(0, NP - 1)], p1_send.at[piece[0]])
        ring_flush(g, piece)
        for r in range(ROUNDS):
            wait_bytes(stage.at[r, pl.ds(0, NP - 1)], p2_send.at[piece[0], r])

    @pl.when(holder)
    def _():
        wait_bytes(gu.at[0, pl.ds(0, 7)], p1_send.at[U[0]])
        ring_flush(gu, U)
        for r in range(ROUNDS):
            wait_bytes(stage_u.at[r, pl.ds(0, NP - 1)], p2_send.at[U[0], r])

    @pl.when(jnp.logical_not(holder))
    def _():
        wait_bytes(gu.at[0, pl.ds(0, 8)], p1_send.at[U[0]])
    for k in range(TILES):
        cross(xt, yt, 1, k).wait_send()
        weights_copy(wa, 0, k).wait_send()
        weights_copy(wb, 1, k).wait_send()
    sums_copy(ra, 0).wait_send()
    sums_copy(rb, 1).wait_send()
    for n in range(2):
        for half in range(2):
            wait_bytes(pa.at[n, pl.ds(0, NP - 1)], ps_send.at[n, half])


def combine(scal_ref, ga_ref, gb_ref, grad_ref, loss_ref):
    grad_ref[...] = 2.0 * (ga_ref[...] - scal_ref[0, 0] * gb_ref[...])
    loss_ref[0, 0] = scal_ref[1, 0]


def body(student, teacher, rounds):
    pairs = float(NZ * NP * TILES * ROWS * ROWS)
    vmem = pl.BlockSpec(memory_space=pltpu.VMEM)
    smem = pl.BlockSpec(memory_space=pltpu.SMEM)
    hbm = pl.BlockSpec(memory_space=pl.ANY)
    dma = pltpu.SemaphoreType.DMA
    part = jax.ShapeDtypeStruct((ROWS, SQ), F32)
    ga, gb, scal = pl.pallas_call(
        functools.partial(kernel, pairs),
        out_shape=(part, part, jax.ShapeDtypeStruct((8, 128), F32)),
        in_specs=[smem, hbm, hbm],
        out_specs=(vmem, vmem, vmem),
        scratch_shapes=[
            pltpu.VMEM((ROWS, SQ), BF16),
            pltpu.VMEM((ROWS, SQ + UQ), BF16),
            pltpu.VMEM((NZ, NP, CR, CC), BF16),
            pltpu.VMEM((NZ, NP, CR, CC), BF16),
            pltpu.VMEM((NZ, NP, VA, CC), BF16),
            pltpu.VMEM((NZ, NP, VB, CC), BF16),
            pltpu.VMEM((ROUNDS, NP, CR, CC), BF16),
            pltpu.VMEM((ROUNDS, NP, CR, CC), BF16),
            pltpu.VMEM((ROUNDS, NP, VA, CC), BF16),
            pltpu.VMEM((ROUNDS, NP, VB, CC), BF16),
            pltpu.VMEM((ROUNDS, ROWS, SQ), BF16),
            pltpu.VMEM((ROUNDS, ROWS, SQ), BF16),
            pltpu.VMEM((ROUNDS, ROWS, UQ), BF16),
            pltpu.VMEM((ROWS, 128), F32),
            pltpu.VMEM((ROWS, 128), F32),
            pltpu.VMEM((TILES, HALF, ROWS), F32),
            pltpu.VMEM((TILES, HALF, ROWS), F32),
            pltpu.VMEM((TILES, HALF, ROWS), F32),
            pltpu.VMEM((TILES, HALF, ROWS), F32),
            pltpu.VMEM((TILES, HALF, ROWS), F32),
            pltpu.VMEM((TILES, HALF, ROWS), F32),
            pltpu.VMEM((TILES, ROWS, ROWS), BF16),
            pltpu.VMEM((TILES, ROWS, ROWS), BF16),
            pltpu.VMEM((ROWS, 128), F32),
            pltpu.VMEM((ROWS, 128), F32),
            pltpu.VMEM((2, 2, 8, 128), F32),
            pltpu.VMEM((2, NP, 8, 128), F32),
            pltpu.VMEM((2, NP, 8, 128), F32),
            dma((2,)),
            dma((4,)), dma((4,)),
            dma((4, 2, PARTS, NZ // 2)), dma((4, 2, PARTS, NZ // 2)),
            dma((4, ROUNDS)), dma((4, ROUNDS)),
            dma((2, TILES)), dma((2, TILES)),
            dma((2, TILES)), dma((2, TILES)),
            dma((2,)), dma((2,)),
            dma((2, 2)), dma((2, 2)),
        ],
        compiler_params=pltpu.CompilerParams(
            collective_id=0, has_side_effects=True, vmem_limit_bytes=60 * 1024 * 1024),
        name="relation",
    )(rounds, student, teacher)
    grad, loss = pl.pallas_call(
        combine,
        out_shape=(part, jax.ShapeDtypeStruct((1, 1), F32)),
        in_specs=[smem, vmem, vmem],
        out_specs=(vmem, smem),
        name="combine",
    )(scal, ga, gb)
    return grad, loss[0, 0]


def solution(mesh):
    return jax.shard_map(
        body,
        mesh=mesh,
        in_specs=(P("rows", "feat"), P("rows", "feat"), P()),
        out_specs=(P("rows", "feat"), P()),
        check_vma=False,
    )
```

time: 133 us -> 126 us (0.947)
  local copies, waits for them, and re-layouts: 3.16 us -> 0 us
  Pallas kernels: 127 us -> 124 us
    pallas_call x1 -> x2, Pallas kernels: 127 us -> 124 us  [the longest x1 122 us: body(): pl.pallas_call(functools.partial(kernel, pairs), out_shape=(part, part, j...]
    unnamed x1 -> x0, local copies, waits for them, and re-layouts: 1.97 us -> none
where the time goes in v2:
time: 126 us; the launch traced here: 125 us
  Pallas kernels  124 us (98%)
    pallas_call x1, Pallas kernels, body(): pl.pallas_call(functools.partial(kernel, pairs), out_shape=(part, part, j...  122 us

profile of v2, /device:TPU:2, one launch (start us, length us, event | category | flops | bytes accessed | tf_op | source)
XLA Modules:
  0.0 124.5 jit_solution(3518406060751605603)
XLA Ops:
  0.6 121.7 %relation.1 = (f32[320,512]{1,0:T(8,128)}, f32[320,512]{1,0:T(8,128)}, f32[8,128]{1,0:T(8,128)}) custom-call(s32[4]{0:T(128)} %rounds_ref.1, bf16[320,512]{1,0:T(8,128)(2,1)} %s_hbm.1, bf16[320,768]{1,0:T(8,128)(2,1)} %t_hbm.1), custom_call_target="tpu_custom_call" | custom-call | tf_op jit(solution)/shard_map/relation/pallas_call | solution.py:436
  122.3 2.2 %combine.1 = (f32[320,512]{1,0:T(8,128)}, f32[1,1]{1,0:T(1,128)}) custom-call(f32[8,128]{1,0:T(8,128)} %get-tuple-element.7.scal_ref, f32[320,512]{1,0:T(8,128)} %get-tuple-element.8.ga_ref, f32[320,512]{1,0:T(8,128)} %get-tuple-element.9.gb_ref), custom_call_target="tpu_custom_call" | custom-call | tf_op jit(solution)/shard_map/combine/pallas_call | solution.py:483

commit v3 on v2

--- a/solution.py
+++ b/solution.py
@@ -21,7 +21,7 @@
 UQ = 256
 VA = 48
 VB = 32
-PARTS = 4
+PARTS = 2
 
 
 def nt_dot(a, b):
@@ -47,9 +47,9 @@
 
 
 def kernel(pairs, rounds_ref, s_hbm, t_hbm, ga_ref, gb_ref, scal_ref,
-           s_ref, t_ref, gs, gu, ga, gb, stage_s, stage_u, stage_a, stage_b, ms, mt, mu,
+           s_ref, t_ref, gs, gr, gu, ga, gb, stage_s, stage_r, stage_u, stage_a, stage_b, ms, mt, mu,
            rn_s, rn_t, ds, dt, xs, xt, ys, yt, wa, wb, ra, rb, pv, pa, pb,
-           in_sem, p1_send, p1_recv, ring_send, ring_recv, p2_send, p2_recv,
+           in_sem, plane_in, p1_send, p1_recv, ring_send, ring_recv, p2_send, p2_recv,
            x_send, x_recv, w_send, w_recv, r_send, r_recv, ps_send, ps_recv):
     load_s = pltpu.make_async_copy(s_hbm, s_ref, in_sem.at[0])
     load_t = pltpu.make_async_copy(t_hbm, t_ref, in_sem.at[1])
@@ -70,29 +70,34 @@
         return {"rows": (q % NZ) * NP + me, "feat": q // NZ}
 
     q_me = core * NZ + z
-    right = {"rows": ((z + 1) % NZ) * NP + me}
-    left = {"rows": ((z + NZ - 1) % NZ) * NP + me}
+    above = ((z + 1) % NZ) * NP
+    below = ((z + NZ - 1) % NZ) * NP
+    right = {"rows": above + me}
+    left = {"rows": below + me}
     mate_core = {"feat": other}
 
     barrier = pltpu.get_barrier_semaphore()
 
     def greet(k, carry):
         pl.semaphore_signal(barrier, inc=1, device_id=plane((me + k) % NP), device_id_type=MESH)
-        pl.semaphore_signal(barrier, inc=1, device_id=line((q_me + k) % NP), device_id_type=MESH)
         return carry
     lax.fori_loop(1, NP, greet, 0)
+    for peer in (right, left, mate_core):
+        pl.semaphore_signal(barrier, inc=1, device_id=peer, device_id_type=MESH)
     load_s.wait()
     rn_s[...] = jnp.broadcast_to(row_norms(s_ref[...]), (ROWS, 128))
     load_t.wait()
     rn_t[...] = jnp.broadcast_to(row_norms(t_ref[...]), (ROWS, 128))
-    pl.semaphore_wait(barrier, 2 * (NP - 1))
-
-    S, U, A, B = (0, 0, 0, CR), (1, SQ, 0, CR), (2, 0, 0, VA), (3, 0, VA, VB)
+    pl.semaphore_wait(barrier, NP + 2)
+    for peer in (right, left):
+        pl.semaphore_signal(plane_in, inc=1, device_id=peer, device_id_type=MESH)
+
+    S, R, U, A, B = (0, 0, VA), (1, VA, VB), (2, 0, CR), (3, 0, VA), (4, VA, VB)
 
     def rect(ref, i, piece, first=0):
-        r0 = pl.multiple_of((i % 4) * CR + piece[2], 16)
+        r0 = pl.multiple_of((i % 4) * CR + piece[1], 16)
         c0 = pl.multiple_of(first + (i // 4) * CC, CC)
-        return ref.at[pl.ds(r0, piece[3]), pl.ds(c0, CC)]
+        return ref.at[pl.ds(r0, piece[2]), pl.ds(c0, CC)]
 
     def scatter(src, g, piece):
         slot = piece[0]
@@ -106,6 +111,19 @@
         lax.fori_loop(1, NP, one, 0)
         pltpu.make_async_copy(rect(src, me, piece), g.at[z, me], p1_recv.at[slot]).start()
 
+    def spread(src, g, piece):
+        slot = piece[0]
+
+        def one(k, carry):
+            d = (me + k) % NP
+            for way, first in ((0, above), (1, below)):
+                pltpu.make_async_remote_copy(
+                    rect(src, d, piece), g.at[z, me],
+                    ring_send.at[slot], ring_recv.at[slot, way, me // (NP // PARTS), 0],
+                    device_id={"rows": first + d}, device_id_type=MESH).start()
+            return carry
+        lax.fori_loop(0, NP, one, 0)
+
     def scatter_u():
         def one(j, carry):
             d = core * 8 + j
@@ -113,14 +131,14 @@
             @pl.when(d != me)
             def _():
                 pltpu.make_async_remote_copy(
-                    rect(t_ref, j, U, SQ), gu.at[z, me], p1_send.at[1], p1_recv.at[1],
+                    rect(t_ref, j, U, SQ), gu.at[z, me], p1_send.at[U[0]], p1_recv.at[U[0]],
                     device_id=plane(d), device_id_type=MESH).start()
             return carry
         lax.fori_loop(0, 8, one, 0)
 
         @pl.when(holder)
         def _():
-            pltpu.make_async_copy(rect(t_ref, me % 8, U, SQ), gu.at[z, me], p1_recv.at[1]).start()
+            pltpu.make_async_copy(rect(t_ref, me % 8, U, SQ), gu.at[z, me], p1_recv.at[U[0]]).start()
 
     def scattered(g, piece):
         wait_bytes(g.at[z], p1_recv.at[piece[0]])
@@ -129,7 +147,7 @@
         block = (z + NZ - step) % NZ if way == 0 else (z + step) % NZ
         ref = g.at[block, pl.ds(part * (NP // PARTS), NP // PARTS)]
         return pltpu.make_async_remote_copy(
-            ref, ref, ring_send.at[slot, way, part, step], ring_recv.at[slot, way, part, step],
+            ref, ref, ring_send.at[slot], ring_recv.at[slot, way, part, step],
             device_id=right if way == 0 else left, device_id_type=MESH)
 
     def ways(part, step):
@@ -146,10 +164,7 @@
                     ring_copy(g, slot, way, part, step).start()
 
     def ring_flush(g, piece):
-        for step in range(NZ // 2):
-            for part in range(PARTS):
-                for way in ways(part, step):
-                    ring_copy(g, piece[0], way, part, step).wait_send()
+        wait_bytes(g.at[pl.ds(0, NZ - 1)], ring_send.at[piece[0]])
 
     def ring_u(step):
         @pl.when(holder)
@@ -170,7 +185,7 @@
             @pl.when(d != me)
             def _():
                 pltpu.make_async_remote_copy(
-                    stage.at[r, d], rect(mate.at[r], i, piece), p2_send.at[slot, r], p2_recv.at[slot, r],
+                    stage.at[r, d], rect(mate.at[r], i, piece), p2_send.at[slot], p2_recv.at[slot, r],
                     device_id=plane(d), device_id_type=MESH).start()
 
             @pl.when(d == me)
@@ -184,7 +199,7 @@
 
     def cross(x, y, side, k):
         return pltpu.make_async_remote_copy(
-            x.at[k], y.at[k], x_send.at[side, k], x_recv.at[side, k],
+            x.at[k], y.at[k], x_send.at[side], x_recv.at[side, k],
             device_id=mate_core, device_id_type=MESH)
 
     def tile_s(k, m):
@@ -247,7 +262,7 @@
     def weights_copy(w, side, k):
         part = w.at[k, own_rows]
         return pltpu.make_async_remote_copy(
-            part, part, w_send.at[side, k], w_recv.at[side, k],
+            part, part, w_send.at[side], w_recv.at[side, k],
             device_id=mate_core, device_id_type=MESH)
 
     def sums_copy(r, side):
@@ -274,6 +289,7 @@
 
     def mate_s(r, carry):
         wait_bytes(stage_s.at[r], p2_recv.at[S[0], r])
+        wait_bytes(stage_r.at[r], p2_recv.at[R[0], r])
         tile_s(r + 1, ms[r])
         return carry
 
@@ -304,6 +320,9 @@
     def deliver_s(r):
         deliver(gs, stage_s, ms, S, r, me)
 
+    def deliver_r(r):
+        deliver(gr, stage_r, ms, R, r, me)
+
     def deliver_a(r):
         deliver(ga, stage_a, mt, A, r, me)
 
@@ -311,56 +330,67 @@
         deliver(gb, stage_b, mt, B, r, me)
 
     scatter(s_ref, gs, S)
-    scattered(gs, S)
-    ring(gs, S, 0)
+    scatter(s_ref, gr, R)
+    pl.semaphore_wait(plane_in, 2)
+    spread(s_ref, gs, S)
+    spread(s_ref, gr, R)
     scatter_u()
     scatter(t_ref, ga, A)
     scatter(t_ref, gb, B)
     tile_s(0, s_ref[...])
-    ring(gs, S, 1)
     tile_u(0, t_ref[:, SQ:SQ + UQ])
     tile_t(0, t_ref[:, 0:SQ])
+    ring(gs, S, 1)
+    ring(gr, R, 1)
     ring(gs, S, 2)
+    ring(gr, R, 2)
+    ring(gs, S, 3)
     ring_u(0)
-    ring(gs, S, 3)
+    ring(gs, S, 4)
+    scattered(gs, S)
+    deliver_s(0)
+    deliver_s(1)
+    ring(gr, R, 3)
+    deliver_s(2)
+    ring_u(1)
+    deliver_s(3)
     scattered(ga, A)
     ring(ga, A, 0)
-    ring_u(1)
-    ring(gs, S, 4)
-    deliver_s(0)
+    ring(gr, R, 4)
+    scattered(gr, R)
+    deliver_r(0)
+    deliver_r(1)
+    ring_u(2)
+    deliver_r(2)
+    deliver_r(3)
     ring(ga, A, 1)
-    deliver_s(1)
-    ring_u(2)
-    deliver_s(2)
+    ring_u(3)
     ring(ga, A, 2)
-    deliver_s(3)
-    ring_u(3)
-    ring(ga, A, 3)
     scattered(gb, B)
     ring(gb, B, 0)
     ring_u(4)
     deliver_u(0)
     deliver_u(1)
-    ring(ga, A, 4)
+    ring(ga, A, 3)
     deliver_u(2)
     ring(gb, B, 1)
     deliver_u(3)
+    lax.fori_loop(0, ROUNDS, mate_s, 0)
+    ring(ga, A, 4)
     deliver_a(0)
+    deliver_a(1)
     ring(gb, B, 2)
-    deliver_a(1)
     deliver_a(2)
+    sum_s = finish(ds, xs, ys, 0)
+    wait_bytes(xs, x_send.at[0])
+    send_sums(rb, 1, lax.fori_loop(0, TILES, inverse, jnp.zeros((HALF, 1), F32)))
     ring(gb, B, 3)
     deliver_a(3)
-    lax.fori_loop(0, ROUNDS, mate_s, 0)
+    lax.fori_loop(0, ROUNDS, mate_u, 0)
+    pull(wb, 1, rb, gb_ref)
     ring(gb, B, 4)
     for r in range(ROUNDS):
         deliver_b(r)
-    lax.fori_loop(0, ROUNDS, mate_u, 0)
-    sum_s = finish(ds, xs, ys, 0)
-    for k in range(TILES):
-        cross(xs, ys, 0, k).wait_send()
-    send_sums(rb, 1, lax.fori_loop(0, TILES, inverse, jnp.zeros((HALF, 1), F32)))
-    pull(wb, 1, rb, gb_ref)
     lax.fori_loop(0, ROUNDS, mate_t, 0)
     sum_t = finish(dt, xt, yt, 1)
 
@@ -394,26 +424,24 @@
     first = lax.broadcasted_iota(jnp.int32, (8, 128), 0) == 0
     scal_ref[...] = jnp.where(first, total_g / (mean_s * pairs), total_h / pairs)
 
-    for g, piece, stage in ((gs, S, stage_s), (ga, A, stage_a), (gb, B, stage_b)):
+    for g, piece, stage in ((gs, S, stage_s), (gr, R, stage_r), (ga, A, stage_a),
+                            (gb, B, stage_b)):
         wait_bytes(g.at[0, pl.ds(0, NP - 1)], p1_send.at[piece[0]])
         ring_flush(g, piece)
-        for r in range(ROUNDS):
-            wait_bytes(stage.at[r, pl.ds(0, NP - 1)], p2_send.at[piece[0], r])
+        wait_bytes(stage.at[:, pl.ds(0, NP - 1)], p2_send.at[piece[0]])
 
     @pl.when(holder)
     def _():
         wait_bytes(gu.at[0, pl.ds(0, 7)], p1_send.at[U[0]])
         ring_flush(gu, U)
-        for r in range(ROUNDS):
-            wait_bytes(stage_u.at[r, pl.ds(0, NP - 1)], p2_send.at[U[0], r])
+        wait_bytes(stage_u.at[:, pl.ds(0, NP - 1)], p2_send.at[U[0]])
 
     @pl.when(jnp.logical_not(holder))
     def _():
         wait_bytes(gu.at[0, pl.ds(0, 8)], p1_send.at[U[0]])
-    for k in range(TILES):
-        cross(xt, yt, 1, k).wait_send()
-        weights_copy(wa, 0, k).wait_send()
-        weights_copy(wb, 1, k).wait_send()
+    wait_bytes(xt, x_send.at[1])
+    wait_bytes(wa.at[:, own_rows], w_send.at[0])
+    wait_bytes(wb.at[:, own_rows], w_send.at[1])
     sums_copy(ra, 0).wait_send()
     sums_copy(rb, 1).wait_send()
     for n in range(2):
@@ -441,11 +469,13 @@
         scratch_shapes=[
             pltpu.VMEM((ROWS, SQ), BF16),
             pltpu.VMEM((ROWS, SQ + UQ), BF16),
-            pltpu.VMEM((NZ, NP, CR, CC), BF16),
+            pltpu.VMEM((NZ, NP, VA, CC), BF16),
+            pltpu.VMEM((NZ, NP, VB, CC), BF16),
             pltpu.VMEM((NZ, NP, CR, CC), BF16),
             pltpu.VMEM((NZ, NP, VA, CC), BF16),
             pltpu.VMEM((NZ, NP, VB, CC), BF16),
-            pltpu.VMEM((ROUNDS, NP, CR, CC), BF16),
+            pltpu.VMEM((ROUNDS, NP, VA, CC), BF16),
+            pltpu.VMEM((ROUNDS, NP, VB, CC), BF16),
             pltpu.VMEM((ROUNDS, NP, CR, CC), BF16),
             pltpu.VMEM((ROUNDS, NP, VA, CC), BF16),
             pltpu.VMEM((ROUNDS, NP, VB, CC), BF16),
@@ -467,12 +497,12 @@
             pltpu.VMEM((2, 2, 8, 128), F32),
             pltpu.VMEM((2, NP, 8, 128), F32),
             pltpu.VMEM((2, NP, 8, 128), F32),
-            dma((2,)),
-            dma((4,)), dma((4,)),
-            dma((4, 2, PARTS, NZ // 2)), dma((4, 2, PARTS, NZ // 2)),
-            dma((4, ROUNDS)), dma((4, ROUNDS)),
-            dma((2, TILES)), dma((2, TILES)),
-            dma((2, TILES)), dma((2, TILES)),
+            dma((2,)), pltpu.SemaphoreType.REGULAR,
+            dma((5,)), dma((5,)),
+            dma((5,)), dma((5, 2, PARTS, NZ // 2)),
+            dma((5,)), dma((5, ROUNDS)),
+            dma((2,)), dma((2, TILES)),
+            dma((2,)), dma((2, TILES)),
             dma((2,)), dma((2,)),
             dma((2, 2)), dma((2, 2)),
         ],

time: 126 us -> 120 us (0.952)
  Pallas kernels: 124 us -> 117 us
    pallas_call x1, Pallas kernels: 122 us -> 115 us  [body(): pl.pallas_call(functools.partial(kernel, pairs), out_shape=(part, part, j...]
where the time goes in v3:
time: 120 us; the launch traced here: 118 us
  Pallas kernels  117 us (98%)
    pallas_call x1, Pallas kernels, body(): pl.pallas_call(functools.partial(kernel, pairs), out_shape=(part, part, j...  115 us

profile of v3, /device:TPU:2, one launch (start us, length us, event | category | flops | bytes accessed | tf_op | source)
XLA Modules:
  0.0 118.1 jit_solution(16174345976658046060)
XLA Ops:
  0.6 115.3 %relation.1 = (f32[320,512]{1,0:T(8,128)}, f32[320,512]{1,0:T(8,128)}, f32[8,128]{1,0:T(8,128)}) custom-call(s32[4]{0:T(128)} %rounds_ref.1, bf16[320,512]{1,0:T(8,128)(2,1)} %s_hbm.1, bf16[320,768]{1,0:T(8,128)(2,1)} %t_hbm.1), custom_call_target="tpu_custom_call" | custom-call | tf_op jit(solution)/shard_map/relation/pallas_call | solution.py:464
  115.9 2.2 %combine.1 = (f32[320,512]{1,0:T(8,128)}, f32[1,1]{1,0:T(1,128)}) custom-call(f32[8,128]{1,0:T(8,128)} %get-tuple-element.7.scal_ref, f32[320,512]{1,0:T(8,128)} %get-tuple-element.8.ga_ref, f32[320,512]{1,0:T(8,128)} %get-tuple-element.9.gb_ref), custom_call_target="tpu_custom_call" | custom-call | tf_op jit(solution)/shard_map/combine/pallas_call | solution.py:513

commit v4 on v3

--- a/solution.py
+++ b/solution.py
@@ -46,7 +46,7 @@
     pltpu.make_async_copy(ref, ref, sem).wait()
 
 
-def kernel(pairs, rounds_ref, s_hbm, t_hbm, ga_ref, gb_ref, scal_ref,
+def kernel(pairs, rounds_ref, s_hbm, t_hbm, ga_hbm, gb_hbm, scal_ref, ga_ref, gb_ref,
            s_ref, t_ref, gs, gr, gu, ga, gb, stage_s, stage_r, stage_u, stage_a, stage_b, ms, mt, mu,
            rn_s, rn_t, ds, dt, xs, xt, ys, yt, wa, wb, ra, rb, pv, pa, pb,
            in_sem, plane_in, p1_send, p1_recv, ring_send, ring_recv, p2_send, p2_recv,
@@ -229,7 +229,7 @@
         return jnp.sum(acc, axis=1, keepdims=True)
 
     def sum_first(n, a, b):
-        first = lax.broadcasted_iota(jnp.int32, (8, 128), 0) == 0
+        first = lax.broadcasted_iota(jnp.int32, (1, 128), 1) == 0
         v = jnp.where(first, a, b)
         pv[n, 0] = v
         pa[n, me] = v
@@ -257,7 +257,7 @@
     def sum_result(n):
         wait_bytes(pb.at[n, pl.ds(0, NP - 1)], ps_recv.at[n, 1])
         v = jnp.sum(pb[n], axis=0)
-        return v[0:1, 0:1], v[1:2, 0:1]
+        return v[:, 0:1], v[:, 1:2]
 
     def weights_copy(w, side, k):
         part = w.at[k, own_rows]
@@ -386,11 +386,13 @@
     send_sums(rb, 1, lax.fori_loop(0, TILES, inverse, jnp.zeros((HALF, 1), F32)))
     ring(gb, B, 3)
     deliver_a(3)
-    lax.fori_loop(0, ROUNDS, mate_u, 0)
-    pull(wb, 1, rb, gb_ref)
     ring(gb, B, 4)
     for r in range(ROUNDS):
         deliver_b(r)
+    lax.fori_loop(0, ROUNDS, mate_u, 0)
+    pull(wb, 1, rb, gb_ref)
+    store_b = pltpu.make_async_copy(gb_ref, gb_hbm, in_sem.at[1])
+    store_b.start()
     lax.fori_loop(0, ROUNDS, mate_t, 0)
     sum_t = finish(dt, xt, yt, 1)
 
@@ -420,10 +422,14 @@
     send_sums(ra, 0, sums)
     sum_second(1)
     pull(wa, 0, ra, ga_ref)
+    store_a = pltpu.make_async_copy(ga_ref, ga_hbm, in_sem.at[0])
+    store_a.start()
     total_h, total_g = sum_result(1)
     first = lax.broadcasted_iota(jnp.int32, (8, 128), 0) == 0
     scal_ref[...] = jnp.where(first, total_g / (mean_s * pairs), total_h / pairs)
 
+    store_a.wait()
+    store_b.wait()
     for g, piece, stage in ((gs, S, stage_s), (gr, R, stage_r), (ga, A, stage_a),
                             (gb, B, stage_b)):
         wait_bytes(g.at[0, pl.ds(0, NP - 1)], p1_send.at[piece[0]])
@@ -465,8 +471,10 @@
         functools.partial(kernel, pairs),
         out_shape=(part, part, jax.ShapeDtypeStruct((8, 128), F32)),
         in_specs=[smem, hbm, hbm],
-        out_specs=(vmem, vmem, vmem),
+        out_specs=(hbm, hbm, vmem),
         scratch_shapes=[
+            pltpu.VMEM((ROWS, SQ), F32),
+            pltpu.VMEM((ROWS, SQ), F32),
             pltpu.VMEM((ROWS, SQ), BF16),
             pltpu.VMEM((ROWS, SQ + UQ), BF16),
             pltpu.VMEM((NZ, NP, VA, CC), BF16),
@@ -494,9 +502,9 @@
             pltpu.VMEM((TILES, ROWS, ROWS), BF16),
             pltpu.VMEM((ROWS, 128), F32),
             pltpu.VMEM((ROWS, 128), F32),
-            pltpu.VMEM((2, 2, 8, 128), F32),
-            pltpu.VMEM((2, NP, 8, 128), F32),
-            pltpu.VMEM((2, NP, 8, 128), F32),
+            pltpu.VMEM((2, 2, 1, 128), F32),
+            pltpu.VMEM((2, NP, 1, 128), F32),
+            pltpu.VMEM((2, NP, 1, 128), F32),
             dma((2,)), pltpu.SemaphoreType.REGULAR,
             dma((5,)), dma((5,)),
             dma((5,)), dma((5, 2, PARTS, NZ // 2)),

time: 120 us -> 118 us (0.983)
    pallas_call x1, Pallas kernels: 115 us -> 114 us  [body(): pl.pallas_call(functools.partial(kernel, pairs), out_shape=(part, part, j...]
where the time goes in v4:
time: 118 us; the launch traced here: 117 us
  Pallas kernels  116 us (98%)
    pallas_call x1, Pallas kernels, body(): pl.pallas_call(functools.partial(kernel, pairs), out_shape=(part, part, j...  114 us

profile of v4, /device:TPU:2, one launch (start us, length us, event | category | flops | bytes accessed | tf_op | source)
XLA Modules:
  0.0 116.8 jit_solution(6869199342252839582)
XLA Ops:
  0.6 114.0 %relation.1 = (f32[320,512]{1,0:T(8,128)}, f32[320,512]{1,0:T(8,128)}, f32[8,128]{1,0:T(8,128)}) custom-call(s32[4]{0:T(128)} %rounds_ref.1, bf16[320,512]{1,0:T(8,128)(2,1)} %s_hbm.1, bf16[320,768]{1,0:T(8,128)(2,1)} %t_hbm.1), custom_call_target="tpu_custom_call" | custom-call | tf_op jit(solution)/shard_map/relation/pallas_call | solution.py:470
  114.6 2.2 %combine.1 = (f32[320,512]{1,0:T(8,128)}, f32[1,1]{1,0:T(1,128)}) custom-call(f32[8,128]{1,0:T(8,128)} %get-tuple-element.7.scal_ref, f32[320,512]{1,0:T(8,128)} %get-tuple-element.8.ga_ref, f32[320,512]{1,0:T(8,128)} %get-tuple-element.9.gb_ref), custom_call_target="tpu_custom_call" | custom-call | tf_op jit(solution)/shard_map/combine/pallas_call | solution.py:521

commit v5 on v4

--- a/solution.py
+++ b/solution.py
@@ -179,7 +179,8 @@
         zz = z ^ (mask // NP)
         low = mask % NP
 
-        def one(d, carry):
+        def one(k, carry):
+            d = (me + k) % NP
             stage[r, d] = g[zz, d ^ low]
 
             @pl.when(d != me)
@@ -192,7 +193,7 @@
             def _():
                 pltpu.make_async_copy(stage.at[r, d], rect(mate.at[r], i, piece), p2_recv.at[slot, r]).start()
             return carry
-        lax.fori_loop(0, NP, one, 0)
+        lax.fori_loop(1, NP + 1, one, 0)
 
     own_rows = pl.ds(pl.multiple_of(core * HALF, 16), HALF)
     far_rows = pl.ds(pl.multiple_of(other * HALF, 16), HALF)

time: 118 us -> 118 us (level)
  no operation moved by 1% of the time
where the time goes in v5:
time: 118 us; the launch traced here: 117 us
  Pallas kernels  116 us (98%)
    pallas_call x1, Pallas kernels, body(): pl.pallas_call(functools.partial(kernel, pairs), out_shape=(part, part, j...  114 us

profile of v5, /device:TPU:2, one launch (start us, length us, event | category | flops | bytes accessed | tf_op | source)
XLA Modules:
  0.0 116.6 jit_solution(12876395076377520396)
XLA Ops:
  0.6 113.7 %relation.1 = (f32[320,512]{1,0:T(8,128)}, f32[320,512]{1,0:T(8,128)}, f32[8,128]{1,0:T(8,128)}) custom-call(s32[4]{0:T(128)} %rounds_ref.1, bf16[320,512]{1,0:T(8,128)(2,1)} %s_hbm.1, bf16[320,768]{1,0:T(8,128)(2,1)} %t_hbm.1), custom_call_target="tpu_custom_call" | custom-call | tf_op jit(solution)/shard_map/relation/pallas_call | solution.py:471
  114.4 2.2 %combine.1 = (f32[320,512]{1,0:T(8,128)}, f32[1,1]{1,0:T(1,128)}) custom-call(f32[8,128]{1,0:T(8,128)} %get-tuple-element.7.scal_ref, f32[320,512]{1,0:T(8,128)} %get-tuple-element.8.ga_ref, f32[320,512]{1,0:T(8,128)} %get-tuple-element.9.gb_ref), custom_call_target="tpu_custom_call" | custom-call | tf_op jit(solution)/shard_map/combine/pallas_call | solution.py:522
